TPU v7x, 128 devices: a whole 4x4x4 slice. The times are simulated.
128 devices in a mesh: rep: 8 (over z_hi, y), shard: 16 (over z_lo, x, core).
Axes of the slice: x: 4, y: 4, z: 4 (z_hi: 2, z_lo: 2; z = z_hi * 2 + z_lo), core: 2. Of those that a mesh axis runs over, the one named last changes fastest.
Arguments:
- residuals: bfloat16 [32, 1024, 4, 1024], P('shard', 'rep'), may hold values from -6 to 6
- lengths: int32 [32], P('shard'), may hold values from 256 to 1024, as said below
- w_query: bfloat16 [1024, 2048], P('shard'), may hold values from -0.1875 to 0.1875
- w_key: bfloat16 [1024, 1024], P('shard'), may hold values from -0.1875 to 0.1875
- w_value: bfloat16 [1024, 1024], P('shard'), may hold values from -0.1875 to 0.1875
- w_out: bfloat16 [2048, 1024], P('shard'), may hold values from -1 to 1
- w_gate: bfloat16 [1024, 3072], P('shard'), may hold values from -0.1875 to 0.1875
- w_up: bfloat16 [1024, 3072], P('shard'), may hold values from -0.1875 to 0.1875
- w_down: bfloat16 [3072, 1024], P('shard'), may hold values from -0.109375 to 0.109375
- attn_gain: float32 [1024], replicated, may hold values from 0.25 to 1.75
- mlp_gain: float32 [1024], replicated, may hold values from 0.25 to 1.75
- query_gain: float32 [128], replicated, may hold values from 0.25 to 1.75
- key_gain: float32 [128], replicated, may hold values from 0.25 to 1.75
- hyper_weight: float32 [2, 6, 1024], replicated, may hold values from -0.09375 to 0.09375
- hyper_static: float32 [2, 4, 6], replicated, may hold values from -3 to 3
- cotangent: bfloat16 [32, 1024, 4, 1024], P('shard', 'rep'), may hold values from -6 to 6
Outputs:
- out_residuals: bfloat16 [32, 1024, 4, 1024], P('shard', 'rep')
- grad_residuals: float32 [32, 1024, 4, 1024], P('shard', 'rep')
- grad_query: float32 [1024, 2048], P('shard')
- grad_key: float32 [1024, 1024], P('shard')
- grad_value: float32 [1024, 1024], P('shard')
- grad_out: float32 [2048, 1024], P('shard')
- grad_gate: float32 [1024, 3072], P('shard')
- grad_up: float32 [1024, 3072], P('shard')
- grad_down: float32 [3072, 1024], P('shard')
- grad_attn_gain: float32 [1024], replicated
- grad_mlp_gain: float32 [1024], replicated
- grad_query_gain: float32 [128], replicated
- grad_key_gain: float32 [128], replicated
- grad_hyper_weight: float32 [2, 6, 1024], replicated
- grad_hyper_static: float32 [2, 4, 6], replicated
Inputs may be any that keep to these rules, and one draw needn't show every extreme that they name: Positions 0 to lengths[b] - 1 of sequence b are its tokens; the rest is padding.
All inputs are finite; a program needn't handle non-finite values.
Results may differ from a plain program's by a relative error of at most 0.025.
Values may be sent and summed in bfloat16 or wider, within the bound.
No kernel may reach another device: no remote copies, remote signals or barrier semaphores. Data moves between devices by JAX's collectives and lax.ppermute only.
A program may use at most 256 MiB of HBM per device.

v0:
```python
from functools import partial

import jax
import jax.numpy as jnp
from jax import lax
from jax.sharding import PartitionSpec as P

EPSILON = 1e-06
ROTARY_BASE = 1000000.0
MASKED = -1e30
CONTRACT_ROWS = (((0,), (0,)), ((), ()))
CONTRACT_COLUMNS = (((1,), (1,)), ((), ()))


def in_one_piece(arrays, axis, dim, along):
    both = jnp.concatenate(arrays, axis=along)
    out, at, gathered = (lax.all_gather(both, axis, axis=dim, tiled=True), 0, [])
    for a in arrays:
        gathered.append(lax.slice_in_dim(out, at, at + a.shape[along], axis=along))
        at += a.shape[along]
    return tuple(gathered)


def rms_scale(values, gain_vec):
    return (
        values * lax.rsqrt(jnp.mean(values * values, axis=-1, keepdims=True) + EPSILON) * gain_vec
    )


def rotary_tables(positions, head_dim):
    half_dim = head_dim // 2
    inverse = ROTARY_BASE ** (-jnp.arange(half_dim, dtype=jnp.float32) * 2.0 / head_dim)
    angles = positions.astype(jnp.float32)[:, None] * inverse[None, :]
    angles = jnp.concatenate([angles, angles], axis=1)
    return (jnp.cos(angles), jnp.sin(angles))


def head_rotary(values, gain_vec, cos_tab, sin_tab, head_count):
    row_count = values.shape[0]
    shaped = rms_scale(values.reshape(row_count, head_count, -1), gain_vec)
    half_dim = shaped.shape[-1] // 2
    turned = jnp.concatenate([-shaped[..., half_dim:], shaped[..., :half_dim]], axis=-1)
    return (shaped * cos_tab[:, None, :] + turned * sin_tab[:, None, :]).reshape(row_count, -1)


def lane_inputs(lanes, mixing, static, gain_vec):
    lane_count = lanes.shape[1]
    normed = lanes * lax.rsqrt(jnp.mean(lanes * lanes, axis=-1, keepdims=True) + EPSILON)
    coeffs = (
        jnp.tanh(jnp.einsum("tsd,kd->tsk", normed, mixing, precision=lax.Precision.HIGHEST))
        + static
    )
    joined = jnp.einsum("ts,tsd->td", coeffs[:, :, 0], lanes, precision=lax.Precision.HIGHEST)
    return (
        rms_scale(joined, gain_vec),
        coeffs[:, :, 1 : 1 + lane_count],
        coeffs[:, :, 1 + lane_count],
    )


def lane_outputs(lanes, mix_coef, out_coef, branch):
    return (
        jnp.einsum("tij,tid->tjd", mix_coef, lanes, precision=lax.Precision.HIGHEST)
        + out_coef[:, :, None] * branch[:, None, :]
    )


def swiglu(gate_act, up_act):
    return jax.nn.silu(gate_act) * up_act


def fold_rows(left_op, pieces):
    running = tuple(
        (jnp.dot(left_op, shard_rows, preferred_element_type=jnp.float32) for shard_rows in pieces)
    )
    stores = tuple((shard_rows for shard_rows in pieces))
    return (running, stores)


def project_rows(grad_low, shard_rows):
    return lax.dot_general(
        grad_low, shard_rows, CONTRACT_COLUMNS, preferred_element_type=jnp.float32
    )


def project_stores(grad_low, stores):
    col_start = 0
    result = None
    for buffer in stores:
        width_here = buffer.shape[1]
        product_part = project_rows(grad_low[:, col_start : col_start + width_here], buffer)
        result = product_part if result is None else result + product_part
        col_start = col_start + width_here
    return result


def on_device(
    residuals,
    lengths,
    w_query,
    w_key,
    w_value,
    w_out,
    w_gate,
    w_up,
    w_down,
    attn_gain,
    mlp_gain,
    query_gain,
    key_gain,
    hyper_weight,
    hyper_static,
    cotangent,
):
    pair_count, seq_dev, lane_count, model_width = residuals.shape
    row_count = pair_count * seq_dev
    seq_len = seq_dev * lax.axis_size("rep")
    head_dim = query_gain.shape[0]
    query_width = w_query.shape[1]
    kv_width = w_key.shape[1]
    ff_width = w_gate.shape[1]
    head_count = query_width // head_dim
    kv_heads = kv_width // head_dim
    group_heads = head_count // kv_heads
    scale_factor = head_dim ** (-0.5)
    local_rows = w_query.shape[0]
    out_factor = query_width // model_width
    down_factor = ff_width // model_width
    places = lax.axis_index("rep") * seq_dev + jnp.arange(seq_dev, dtype=jnp.int32)
    positions = jnp.repeat(places, pair_count)
    valid_rows = (places[:, None] < lengths[None, :]).astype(jnp.float32).reshape(row_count)
    cos_tab, sin_tab = rotary_tables(positions, head_dim)
    lanes_zero = (
        residuals.astype(jnp.float32)
        .transpose(1, 0, 2, 3)
        .reshape(row_count, lane_count, model_width)
    )
    (normed_one, mix_one, out_one), pull_pre_one = jax.vjp(
        lane_inputs, lanes_zero, hyper_weight[0], hyper_static[0], attn_gain
    )
    normed_one_low = normed_one.astype(jnp.bfloat16)
    (query_acc, key_acc, value_acc), in_stores = fold_rows(
        normed_one_low,
        (
            lax.all_gather(w_query, "shard", axis=0, tiled=True),
            lax.all_gather(w_key, "shard", axis=0, tiled=True),
            lax.all_gather(w_value, "shard", axis=0, tiled=True),
        ),
    )
    query_rot, pull_query = jax.vjp(
        partial(head_rotary, cos_tab=cos_tab, sin_tab=sin_tab, head_count=head_count),
        query_acc,
        query_gain,
    )
    key_rot, pull_key = jax.vjp(
        partial(head_rotary, cos_tab=cos_tab, sin_tab=sin_tab, head_count=kv_heads),
        key_acc,
        key_gain,
    )
    query_low = query_rot.astype(jnp.bfloat16).reshape(
        seq_dev, pair_count, kv_heads, group_heads, head_dim
    )
    key_local = key_rot.astype(jnp.bfloat16).reshape(seq_dev, pair_count, kv_width)
    value_local = value_acc.astype(jnp.bfloat16).reshape(seq_dev, pair_count, kv_width)
    key_value = lax.all_gather(
        jnp.stack([key_local, value_local], axis=2), "rep", axis=0, tiled=True
    )
    key_heads = key_value[:, :, 0].reshape(seq_len, pair_count, kv_heads, head_dim)
    value_heads = key_value[:, :, 1].reshape(seq_len, pair_count, kv_heads, head_dim)
    key_places = jnp.arange(seq_len, dtype=jnp.int32)
    allowed = (key_places[None, None, :] <= places[None, :, None]) & (
        key_places[None, None, :] < lengths[:, None, None]
    )
    allowed = allowed[:, None, None, :, :]
    scores = (
        jnp.einsum("sbkgd,pbkd->bkgsp", query_low, key_heads, preferred_element_type=jnp.float32)
        * scale_factor
    )
    scores = jnp.where(allowed, scores, MASKED)
    attn_probs = jnp.exp(scores - jnp.max(scores, axis=-1, keepdims=True))
    attn_probs = attn_probs / jnp.sum(attn_probs, axis=-1, keepdims=True)
    prob_low = attn_probs.astype(jnp.bfloat16)
    attended = jnp.einsum(
        "bkgsp,pbkd->sbkgd", prob_low, value_heads, preferred_element_type=jnp.float32
    )
    attended_low = attended.reshape(row_count, query_width).astype(jnp.bfloat16)
    (branch_one,), out_stores = fold_rows(
        attended_low, (lax.all_gather(w_out, "shard", axis=0, tiled=True),)
    )
    lanes_one, pull_post_one = jax.vjp(lane_outputs, lanes_zero, mix_one, out_one, branch_one)
    (normed_two, mix_two, out_two), pull_pre_two = jax.vjp(
        lane_inputs, lanes_one, hyper_weight[1], hyper_static[1], mlp_gain
    )
    normed_two_low = normed_two.astype(jnp.bfloat16)
    (gate_acc, up_acc), mlp_stores = fold_rows(
        normed_two_low, in_one_piece((w_gate, w_up), "shard", 0, 1)
    )
    hidden_act, pull_swiglu = jax.vjp(swiglu, gate_acc, up_acc)
    hidden_low = hidden_act.astype(jnp.bfloat16)
    (branch_two,), down_stores = fold_rows(
        hidden_low, (lax.all_gather(w_down, "shard", axis=0, tiled=True),)
    )
    lanes_two, pull_post_two = jax.vjp(lane_outputs, lanes_one, mix_two, out_two, branch_two)
    out_residuals = (
        lanes_two.reshape(seq_dev, pair_count, lane_count, model_width)
        .transpose(1, 0, 2, 3)
        .astype(jnp.bfloat16)
    )
    tangent = (
        cotangent.astype(jnp.float32)
        .transpose(1, 0, 2, 3)
        .reshape(row_count, lane_count, model_width)
        * valid_rows[:, None, None]
    )
    grad_one_a, grad_mix_two, grad_out_two, grad_branch_two = pull_post_two(tangent)
    branch_two_low = grad_branch_two.astype(jnp.bfloat16)
    hidden_grad = project_stores(branch_two_low, down_stores)
    grad_gate_act, grad_up_act = pull_swiglu(hidden_grad)
    gate_up_low = jnp.concatenate([grad_gate_act, grad_up_act], axis=1).astype(jnp.bfloat16)
    normed_two_grad = project_stores(gate_up_low, mlp_stores)
    grad_one_b, grad_hyper_w_two, grad_hyper_s_two, grad_mlp_gain = pull_pre_two(
        (normed_two_grad, grad_mix_two, grad_out_two)
    )
    grad_zero_a, grad_mix_one, grad_out_one, grad_branch_one = pull_post_one(
        grad_one_a + grad_one_b
    )
    branch_one_low = grad_branch_one.astype(jnp.bfloat16)
    attended_grad = project_stores(branch_one_low, out_stores)
    attended_grad_low = attended_grad.astype(jnp.bfloat16).reshape(
        seq_dev, pair_count, kv_heads, group_heads, head_dim
    )
    prob_grad = jnp.einsum(
        "sbkgd,pbkd->bkgsp", attended_grad_low, value_heads, preferred_element_type=jnp.float32
    )
    score_grad = (
        attn_probs * (prob_grad - jnp.sum(attn_probs * prob_grad, axis=-1, keepdims=True))
    ).astype(jnp.bfloat16)
    query_rot_grad = (
        jnp.einsum(
            "bkgsp,pbkd->sbkgd", score_grad, key_heads, preferred_element_type=jnp.float32
        ).reshape(row_count, query_width)
        * scale_factor
    )
    row_span = lax.axis_size("rep") * seq_dev
    key_part = (
        jnp.einsum("bkgsp,sbkgd->pbkd", score_grad, query_low, preferred_element_type=jnp.float32)
        * scale_factor
    )
    value_part = jnp.einsum(
        "bkgsp,sbkgd->pbkd", prob_low, attended_grad_low, preferred_element_type=jnp.float32
    )
    kv_grad = lax.psum_scatter(
        jnp.stack(
            [
                key_part.reshape(row_span, pair_count, kv_width),
                value_part.reshape(row_span, pair_count, kv_width),
            ],
            axis=2,
        ).astype(jnp.bfloat16),
        "rep",
        scatter_dimension=0,
        tiled=True,
    ).astype(jnp.float32)
    key_rot_grad = kv_grad[:, :, 0].reshape(row_count, kv_width)
    value_grad = kv_grad[:, :, 1].reshape(row_count, kv_width)
    query_acc_grad, grad_query_gain = pull_query(query_rot_grad)
    key_acc_grad, grad_key_gain = pull_key(key_rot_grad)
    qkv_low = jnp.concatenate([query_acc_grad, key_acc_grad, value_grad], axis=1).astype(
        jnp.bfloat16
    )
    normed_one_grad = project_stores(qkv_low, in_stores)
    grad_zero_b, grad_hyper_w_one, grad_hyper_s_one, grad_attn_gain = pull_pre_one(
        (normed_one_grad, grad_mix_one, grad_out_one)
    )
    grad_residuals = (
        (grad_zero_a + grad_zero_b)
        .reshape(seq_dev, pair_count, lane_count, model_width)
        .transpose(1, 0, 2, 3)
    )
    qkv_edge = query_width + 2 * kv_width
    gate_up_edge = 2 * ff_width
    attn_part = jnp.concatenate(
        [
            lax.dot_general(
                normed_one_low, qkv_low, CONTRACT_ROWS, preferred_element_type=jnp.float32
            ),
            lax.dot_general(
                attended_low, branch_one_low, CONTRACT_ROWS, preferred_element_type=jnp.float32
            ).reshape(lax.axis_size("shard") * local_rows, out_factor * model_width),
        ],
        axis=1,
    )
    mlp_part = jnp.concatenate(
        [
            lax.dot_general(
                normed_two_low, gate_up_low, CONTRACT_ROWS, preferred_element_type=jnp.float32
            ),
            lax.dot_general(
                hidden_low, branch_two_low, CONTRACT_ROWS, preferred_element_type=jnp.float32
            ).reshape(lax.axis_size("shard") * local_rows, down_factor * model_width),
        ],
        axis=1,
    )
    owned = lax.psum_scatter(
        jnp.concatenate(
            [
                attn_part[:, :qkv_edge],
                mlp_part[:, :gate_up_edge],
                attn_part[:, qkv_edge:],
                mlp_part[:, gate_up_edge:],
            ],
            axis=1,
        ).astype(jnp.bfloat16),
        "shard",
        scatter_dimension=0,
        tiled=True,
    )
    summed = lax.psum(owned, "rep").astype(jnp.float32)
    edge_key = query_width + kv_width
    edge_value = edge_key + kv_width
    edge_gate = edge_value + ff_width
    edge_up = edge_gate + ff_width
    edge_out = edge_up + query_width
    grad_query = summed[:, :query_width]
    grad_key = summed[:, query_width:edge_key]
    grad_value = summed[:, edge_key:edge_value]
    grad_gate = summed[:, edge_value:edge_gate]
    grad_up = summed[:, edge_gate:edge_up]
    grad_out = summed[:, edge_up:edge_out].reshape(local_rows * out_factor, model_width)
    grad_down = summed[:, edge_out:].reshape(local_rows * down_factor, model_width)
    small_sums = lax.psum(
        (
            grad_attn_gain,
            grad_mlp_gain,
            grad_query_gain,
            grad_key_gain,
            jnp.stack([grad_hyper_w_one, grad_hyper_w_two]),
            jnp.stack([grad_hyper_s_one, grad_hyper_s_two]),
        ),
        ("rep", "shard"),
    )
    return (
        out_residuals,
        grad_residuals,
        grad_query,
        grad_key,
        grad_value,
        grad_out,
        grad_gate,
        grad_up,
        grad_down,
        small_sums[0],
        small_sums[1],
        small_sums[2],
        small_sums[3],
        small_sums[4],
        small_sums[5],
    )


def solution(mesh):
    in_specs = (
        P("shard", "rep", None, None),
        P("shard"),
        P("shard", None),
        P("shard", None),
        P("shard", None),
        P("shard", None),
        P("shard", None),
        P("shard", None),
        P("shard", None),
        P(),
        P(),
        P(),
        P(),
        P(),
        P(),
        P("shard", "rep", None, None),
    )
    out_specs = (
        P("shard", "rep", None, None),
        P("shard", "rep", None, None),
        P("shard", None),
        P("shard", None),
        P("shard", None),
        P("shard", None),
        P("shard", None),
        P("shard", None),
        P("shard", None),
        P(),
        P(),
        P(),
        P(),
        P(),
        P(),
    )
    return jax.shard_map(
        on_device, mesh=mesh, in_specs=in_specs, out_specs=out_specs, check_vma=False
    )
```

profile of v0, /device:TPU:0, one launch (start us, length us, event | category | flops | bytes accessed | tf_op | source)
XLA Modules:
  0.0 1006.1 jit_solution(9935309786682353168)
XLA Ops:
  16.6 6.7 broadcast_add_fusion.1
  28.2 5.6 fusion.122
  35.1 11.1 %all-gather.8.cloned.1.call-done = bf16[1024,1024]{1,0:T(8,128)(2,1)} async-done(((bf16[64,1024]{1,0:T(8,128)(2,1)}), bf16[1024,1024]{1,0:T(8,128)(2,1)}) %all-gather.8.cloned.1.call-update) | async-done | bytes 2097168 | tf_op jit(solution)/shard_map/all_gather | solution.py:146
  53.2 29.0 %all-gather.10.cloned.1.call-done = bf16[1024,1024]{1,0:T(8,128)(2,1)} async-done(((bf16[64,1024]{1,0:T(8,128)(2,1)}), bf16[1024,1024]{1,0:T(8,128)(2,1)}) %all-gather.10.cloned.1.call-update) | async-done | bytes 2097168 | tf_op jit(solution)/shard_map/all_gather | solution.py:147
  102.3 3.0 bitcast_multiply_fusion.2
  105.3 16.0 %all-gather.14.cloned.1.call-done = bf16[1024,2048]{1,0:T(8,128)(2,1)} async-done(((bf16[64,2048]{1,0:T(8,128)(2,1)}), bf16[1024,2048]{1,0:T(8,128)(2,1)}) %all-gather.14.cloned.1.call-update) | async-done | bytes 4194320 | tf_op jit(solution)/shard_map/all_gather | solution.py:145
  121.3 3.4 fusion.124
  130.6 3.2 fusion.41
  135.7 109.1 %all-gather.12.cloned.1.call-done = bf16[1024,2,2,1024]{0,3,1,2:T(8,128)(2,1)} async-done(((bf16[128,2,2,1024]{0,3,1,2:T(8,128)(2,1)}), bf16[1024,2,2,1024]{0,3,1,2:T(8,128)(2,1)}) %all-gather.12.cloned.1.call-update) | async-done | bytes 8388624 | tf_op jit(solution)/shard_map/all_gather | solution.py:165
  244.7 6.0 fusion.111
  250.7 10.5 %fusion.121 = (f32[2,8,2,128]{3,2,1,0:T(2,128)S(1)}, f32[2,8,2,128,1024]{3,4,2,1,0:T(8,128)}) fusion(pred[2,128,1024]{1,2,0:T(8,128)(4,1)S(1)} %copy-done.74, bf16[1024,2,8,128,1]{0,3,4,2,1:T(8,128)(2,1)} %bitcast.293, bf16[128,2,8,2,128]{0,4,3,2,1:T(8,128)(2,1)S(1)} %copy.397), kind=kOutput, calls=%fused_computation.229 | convolution fusion | flops 1090520064 | bytes 22298624 | tf_op jit(solution)/shard_map/sub | solution.py:180
  261.3 8.8 fusion.53
  272.2 10.3 %all-gather.16.cloned.1.call-done = bf16[2048,1024]{1,0:T(8,128)(2,1)} async-done(((bf16[128,1024]{1,0:T(8,128)(2,1)}), bf16[2048,1024]{1,0:T(8,128)(2,1)}) %all-gather.16.cloned.1.call-update) | async-done | bytes 4194320 | tf_op jit(solution)/shard_map/all_gather | solution.py:188
  282.4 3.6 fusion.125
  286.1 7.4 multiply_reduce_fusion.6
  293.7 3.1 broadcast_multiply_fusion.1
  298.8 6.7 broadcast_add_fusion
  306.5 17.9 %fusion.128 = f32[256,4,4]{2,1,0:T(4,128)S(1)} fusion(f32[256,4,1024]{2,1,0:T(4,128)} %get-tuple-element.182, f32[256,4,1024]{2,1,0:T(4,128)} %bitcast_multiply_fusion.2), kind=kOutput, calls=%fused_computation.236 | convolution fusion | flops 50331648 | bytes 8404992 | tf_op jit(solution)/shard_map/transpose(jvp(tij,tid->tjd))/dot_general | solution.py:63
  325.6 9.6 fusion.126
  335.5 21.0 %all-gather.18.cloned.1.call-done = bf16[1024,6144]{1,0:T(8,128)(2,1)} async-done(((bf16[64,6144]{1,0:T(8,128)(2,1)}), bf16[1024,6144]{1,0:T(8,128)(2,1)}) %all-gather.18.cloned.1.call-update) | async-done | bytes 12582928 | tf_op jit(solution)/shard_map/all_gather | solution.py:17
  356.5 4.7 fusion.15
  362.9 6.9 multiply_convert_fusion.1
  369.8 31.6 %all-gather.20.cloned.1.call-done = bf16[3072,1024]{1,0:T(8,128)(2,1)} async-done(((bf16[192,1024]{1,0:T(8,128)(2,1)}), bf16[3072,1024]{1,0:T(8,128)(2,1)}) %all-gather.20.cloned.1.call-update) | async-done | bytes 6291472 | tf_op jit(solution)/shard_map/all_gather | solution.py:201
  401.3 5.6 fusion.127
  406.9 3.0 mul.663
  411.5 4.9 multiply_reduce_fusion.4
  417.2 9.3 fusion.33
  426.6 5.7 fusion.9
  432.4 5.7 multiply_reduce_fusion.12
  438.5 16.6 %fusion.78 = f32[256,1,4]{2,1,0:T(1,128)S(1)} fusion(f32[256,4,1024]{2,1,0:T(4,128)S(1)} %copy-done, f32[256,1024,1]{1,0,2:T(8,128)S(1)} %bitcast.325), kind=kOutput, calls=%fused_computation.134 | convolution fusion | flops 12582912 | bytes 5246976 | tf_op jit(solution)/shard_map/transpose(jvp(ts,tsd->td))/dot_general | solution.py:53
  455.3 3.5 fusion.87
  460.8 2.8 multiply_reduce_fusion.3
  464.0 19.6 %multiply_reduce_fusion.1 = (f32[256,4]{1,0:T(8,128)}, bf16[256,1024]{1,0:T(8,128)(2,1)S(1)}, f32[256,4,1024]{2,1,0:T(4,128)}) fusion(f32[256,1024]{1,0:T(8,128)} %copy-done.117, f32[256,4]{1,0:T(8,128)S(1)} %bitcast.337, f32[256,4,1024]{2,1,0:T(4,128)} %get-tuple-element.182, f32[256,4]{1,0:T(8,128)S(1)} %copy.387, f32[256,4]{1,0:T(8,128)S(1)} %copy.367, ...), kind=kOutput, calls=%fused_computation.43 | convolution fusion | flops 61602816 | bytes 19435520 | tf_op jit(solution)/shard_map/transpose(jvp(tij,tid->tjd))/dot_general | solution.py:63
  487.5 12.3 %fusion.1 = (f32[2,8,2,128]{3,2,1,0:T(2,128)S(1)}, f32[2,8,1024,128,2]{3,2,4,1,0:T(8,128)}) fusion(f32[2,8,2,128,1024]{3,4,2,1,0:T(8,128)} %get-tuple-element.180, f32[2,8,2,128]{3,2,1,0:T(2,128)S(1)} %copy-done.98, bf16[1024,2,8,128,1]{0,3,4,2,1:T(8,128)(2,1)} %bitcast.316, bf16[128,2,8,2,128]{0,4,3,2,1:T(8,128)(2,1)S(1)} %copy.399), kind=kOutput, calls=%fused_computation.4 | convolution fusion | flops 1086320640 | bytes 38830080 | tf_op jit(solution)/shard_map/sbkgd,pbkd->bkgsp/dot_general | solution.py:232
  499.8 10.6 %bitcast_convert_fusion = bf16[2,8,128,1024]{3,2,1,0:T(8,128)(2,1)} fusion(bf16[128,2,8,2,128]{0,4,3,2,1:T(8,128)(2,1)S(1)} %copy.399, f32[2,8,2,128,1024]{3,4,2,1,0:T(8,128)} %get-tuple-element.180, f32[2,8,2,128]{3,2,1,0:T(2,128)S(1)} %copy-done.98), kind=kOutput, calls=%fused_computation.13 | convolution fusion | flops 1084227584 | bytes 22036480 | tf_op jit(solution)/shard_map/bkgsp,sbkgd->pbkd/dot_general | solution.py:249
  510.4 11.7 %fusion.3 = bf16[2,8,2,128,1024]{3,4,2,1,0:T(8,128)(2,1)S(1)} fusion(f32[2,8,1024,128,2]{3,2,4,1,0:T(8,128)} %get-tuple-element.190, f32[2,8,2,128]{3,2,1,0:T(2,128)S(1)} %get-tuple-element.189, f32[2,8,2,128,1024]{3,4,2,1,0:T(8,128)} %get-tuple-element.180, f32[2,8,2,128]{3,2,1,0:T(2,128)S(1)} %copy-done.98), kind=kLoop, calls=%fused_computation.6 | loop fusion | flops 16777216 | bytes 41975808 | tf_op jit(solution)/shard_map/convert_element_type | solution.py:237
  522.2 4.8 fusion.5
  527.0 11.3 %copy.401 = bf16[1024,2,1,1024]{3,1,0,2:T(2,128)(2,1)} copy(bf16[1024,2,1,1024]{0,3,1,2:T(8,128)(2,1)} %bitcast.296) | data formatting | bytes 8388608 | tf_op jit(solution)/shard_map/stack;reshape | solution.py:253
  538.3 11.4 %copy.402 = bf16[1024,2,1,1024]{3,1,0,2:T(2,128)(2,1)} copy(bf16[1024,2,1,1024]{0,3,1,2:T(8,128)(2,1)} %bitcast.308) | data formatting | bytes 8388608 | tf_op jit(solution)/shard_map/stack;reshape | solution.py:253
  549.7 10.0 copy_bitcast_fusion
  559.6 14.4 %reshape.443 = bf16[1024,4096]{1,0:T(8,128)(2,1)} reshape(bf16[1024,2,2,1024]{3,2,1,0:T(2,128)(2,1)} %copy_bitcast_fusion) | data formatting | bytes 16777216
  574.1 7.1 convolution_bitcast_fusion
  585.1 3.3 multiply_reduce_fusion.8
  588.6 3.4 fusion.40
  594.4 3.3 convolution_convert_fusion.3
  597.7 7.3 reshape.415
  605.0 4.4 convolution_convert_fusion.2
  609.5 10.6 %reshape.416 = bf16[1024,3072]{1,0:T(8,128)(2,1)} reshape(bf16[3072,1024]{1,0:T(8,128)(2,1)} %convolution_convert_fusion.2) | data formatting | bytes 12582912 | tf_op jit(solution)/shard_map/reshape | solution.py:300
  620.0 8.2 convolution_convert_fusion
  628.3 61.3 %reduce-scatter.8.cloned.1.call-done = bf16[128,4096]{1,0:T(8,128)(2,1)} async-done(((bf16[1024,4096]{1,0:T(8,128)(2,1)}), bf16[128,4096]{1,0:T(8,128)(2,1)}) %reduce-scatter.8.cloned.1.call-update) | async-done | bytes 1048592
  699.1 7.4 convolution_convert_fusion.1
  706.5 19.8 %pad_maximum_fusion = bf16[1024,15360]{1,0:T(8,128)(2,1)} fusion(bf16[1024,3072]{1,0:T(8,128)(2,1)} %reshape.416, bf16[1024,2048]{1,0:T(8,128)(2,1)S(1)} %copy-done.16, bf16[1024,6144]{1,0:T(8,128)(2,1)} %convolution_convert_fusion, bf16[1024,4096]{1,0:T(8,128)(2,1)} %convolution_convert_fusion.1), kind=kLoop, calls=%fused_computation.1 | loop fusion | flops 125829120 | bytes 62914560 | tf_op jit(solution)/shard_map/concatenate | solution.py:305
  729.2 3.0 copy.411
  732.4 11.5 %fusion.129 = f32[256,4,4]{1,2,0:T(4,128)S(1)} fusion(f32[256,4,1024]{2,1,0:T(4,128)} %get-tuple-element.188, bf16[256,4,1024]{2,1,0:T(4,128)(2,1)} %bitcast.318), kind=kOutput, calls=%fused_computation.237 | convolution fusion | flops 50331648 | bytes 6307840 | tf_op jit(solution)/shard_map/transpose(jvp(tij,tid->tjd))/dot_general | solution.py:63
  744.2 12.2 %add_convert_fusion = bf16[256,4,1024]{2,1,0:T(4,128)(2,1)S(1)} fusion(f32[256,4,4]{2,1,0:T(4,128)S(1)} %copy-done.51, f32[256,4,1024]{2,1,0:T(4,128)} %get-tuple-element.182, f32[256,1024]{1,0:T(8,128)S(1)} %copy-done.25, f32[256,4]{1,0:T(8,128)S(1)} %bitcast.323), kind=kOutput, calls=%fused_computation.48 | convolution fusion | flops 53477376 | bytes 7360512 | tf_op jit(solution)/shard_map/jvp(tij,tid->tjd)/dot_general | solution.py:63
  758.6 4.4 fusion.62
  768.3 8.2 fusion.80
  776.7 3.5 fusion.88
  785.2 111.6 %reduce-scatter.6.cloned.1.call-done = bf16[64,15360]{1,0:T(8,128)(2,1)} async-done(((bf16[1024,15360]{1,0:T(8,128)(2,1)}), bf16[64,15360]{1,0:T(8,128)(2,1)}) %reduce-scatter.6.cloned.1.call-update) | async-done | bytes 1966096 | tf_op jit(solution)/shard_map/reduce_scatter | solution.py:304
  897.0 3.0 broadcast_multiply_fusion
  900.1 4.6 fusion.68
  904.7 69.7 %all-reduce.10 = (f32[1024]{0:T(1024)}, f32[1024]{0:T(1024)}, f32[128]{0:T(128)}, f32[128]{0:T(128)}, f32[2,6,1024]{2,1,0:T(8,128)S(1)}, /*index=5*/f32[2,4,6]{2,1,0:T(4,128)}) all-reduce(f32[1024]{0:T(1024)S(1)} %get-tuple-element.128, f32[1024]{0:T(1024)S(1)} %copy-done.112, ...), channel_id=1, replica_groups=mesh['rep'=8,'shard'=16] {'rep','shard'}, use_global_device_ids=true, to_apply=%region_23.24 | all-reduce | flops 14640 | bytes 117120 | tf_op jit(solution)/shard_map/psum | solution.py:331
  975.2 14.4 %fusion.18 = f32[256,4,1024]{2,1,0:T(4,128)S(1)} fusion(f32[256,4,1024]{2,1,0:T(4,128)} %bitcast.286, f32[256,4,1024]{2,0,1:T(8,128)} %copy-done.10, f32[256,4,4]{2,1,0:T(4,128)S(1)} %copy-done.41, f32[256,4,1024]{2,1,0:T(4,128)} %get-tuple-element.188, f32[256,4]{1,0:T(8,128)S(1)} %copy.415, f32[256,4]{1,0:T(8,128)S(1)} %copy.409, ...), kind=kOutput, calls=%fused_computation.34 | convolution fusion | flops 57671680 | bytes 17854464 | tf_op jit(solution)/shard_map/transpose(jvp(tij,tid->tjd))/dot_general | solution.py:63
  989.6 3.0 copy.531
  (398 shorter events, 106.6 us)
Async XLA Ops:
  7.2 5.9 copy-start.11
  7.2 39.1 %all-gather.8.cloned.1.call-start = ((), (), s32[]{:S(2)}) async-start(), calls=%async_computation.2 | async-start | bytes 2228224 | tf_op jit(solution)/shard_map/all_gather | solution.py:146
  7.9 74.2 %all-gather.10.cloned.1.call-start = ((), (), s32[]{:S(2)}) async-start(), calls=%async_computation.3 | async-start | bytes 2228224 | tf_op jit(solution)/shard_map/all_gather | solution.py:147
  8.7 112.6 %all-gather.14.cloned.1.call-start = ((), (), s32[]{:S(2)}) async-start(), calls=%async_computation.5 | async-start | bytes 4456448 | tf_op jit(solution)/shard_map/all_gather | solution.py:145
  9.4 235.3 %all-gather.12.cloned.1.call-start = ((), (), s32[]{:S(2)}) async-start(), calls=%async_computation.4 | async-start | bytes 9437184 | tf_op jit(solution)/shard_map/all_gather | solution.py:165
  16.6 7.3 copy-start.65
  24.0 9.8 copy-start.58
  26.6 8.2 copy-start.109
  26.6 8.3 copy-start.93
  28.2 100.8 %copy-start.38 = (f32[256,128]{1,0:T(8,128)}, f32[256,128]{1,0:T(8,128)S(1)}, u32[]{:S(2)}) copy-start(f32[256,128]{1,0:T(8,128)S(1)} %get-tuple-element.163) | copy-start | bytes 393220
  28.2 102.1 %copy-start.36 = (f32[256,128]{1,0:T(8,128)}, f32[256,128]{1,0:T(8,128)S(1)}, u32[]{:S(2)}) copy-start(f32[256,128]{1,0:T(8,128)S(1)} %get-tuple-element.164) | copy-start | bytes 393220
  34.8 14.0 %copy-start.101 = (f32[256]{0:T(256)}, f32[256]{0:T(256)S(1)}, u32[]{:S(2)}) copy-start(f32[256]{0:T(256)S(1)} %fusion.94) | copy-start | bytes 3076
  35.1 86.1 %copy-start.47 = (bf16[256,1024]{1,0:T(8,128)(2,1)}, bf16[256,1024]{1,0:T(8,128)(2,1)S(1)}, u32[]{:S(2)}) copy-start(bf16[256,1024]{1,0:T(8,128)(2,1)S(1)} %multiply_convert_fusion.3) | copy-start | bytes 1572868
  84.4 7.2 copy-start.83
  84.7 13.9 %copy-start.17 = (bf16[2,128,4,1024]{3,2,1,0:T(4,128)(2,1)S(1)}, bf16[2,128,4,1024]{3,2,1,0:T(4,128)(2,1)}, u32[]{:S(2)}) copy-start(bf16[2,128,4,1024]{3,2,1,0:T(4,128)(2,1)} %param.31) | copy-start | bytes 6291460
  88.1 194.3 %all-gather.16.cloned.1.call-start = ((), (), s32[]{:S(2)}) async-start(), calls=%async_computation.6 | async-start | bytes 4456448 | tf_op jit(solution)/shard_map/all_gather | solution.py:188
  88.7 267.7 %all-gather.18.cloned.1.call-start = ((), (), s32[]{:S(2)}) async-start(), calls=%async_computation.7 | async-start | bytes 13369344 | tf_op jit(solution)/shard_map/all_gather | solution.py:17
  90.9 310.5 %all-gather.20.cloned.1.call-start = ((), (), s32[]{:S(2)}) async-start(), calls=%async_computation.8 | async-start | bytes 6684672 | tf_op jit(solution)/shard_map/all_gather | solution.py:201
  91.6 597.9 %reduce-scatter.8.cloned.1.call-start = ((), (), s32[]{:S(2)}) async-start(), calls=%async_computation.11 | async-start | bytes 9437184
  96.1 189.9 %copy-start.40 = (f32[256,4,4]{2,1,0:T(4,128)}, f32[256,4,4]{2,1,0:T(4,128)S(1)}, u32[]{:S(2)}) copy-start(f32[256,4,4]{2,1,0:T(4,128)S(1)} %copy.388) | copy-start | bytes 49156
  135.7 115.1 %copy-start.28 = (bf16[128,2,8,2,128]{0,4,3,2,1:T(8,128)(2,1)}, bf16[128,2,8,2,128]{0,4,3,2,1:T(8,128)(2,1)S(1)}, u32[]{:S(2)}) copy-start(bf16[128,2,8,2,128]{0,4,3,2,1:T(8,128)(2,1)S(1)} %copy.397) | copy-start | bytes 3145732
  135.7 115.1 %copy-start.74 = (pred[2,128,1024]{1,2,0:T(8,128)(4,1)S(1)}, pred[2,128,1024]{1,2,0:T(8,128)(4,1)}, u32[]{:S(2)}) copy-start(pred[2,128,1024]{1,2,0:T(8,128)(4,1)} %broadcast_and_fusion) | copy-start | bytes 786436
  261.3 8.8 copy-start.97
  272.1 21.3 %copy-start.23 = (bf16[256,2048]{1,0:T(8,128)(2,1)}, bf16[256,2048]{1,0:T(8,128)(2,1)S(1)}, u32[]{:S(2)}) copy-start(bf16[256,2048]{1,0:T(8,128)(2,1)S(1)} %convert_element_type.103) | copy-start | bytes 3145732
  272.2 13.9 %copy-start.79 = (f32[256,4,1]{1,0,2:T(8,128)S(1)}, f32[256,4,1]{1,0,2:T(8,128)}, u32[]{:S(2)}) copy-start(f32[256,4,1]{1,0,2:T(8,128)} %copy.438) | copy-start | bytes 12292
  286.0 7.4 copy-start.117
  305.6 20.0 %copy-start.63 = (f32[256,4,1]{1,0,2:T(8,128)}, f32[256,4,1]{1,0,2:T(8,128)S(1)}, u32[]{:S(2)}) copy-start(f32[256,4,1]{1,0,2:T(8,128)S(1)} %copy.443) | copy-start | bytes 12292
  324.3 32.1 %copy-start.75 = (f32[1024]{0:T(1024)S(1)}, f32[1024]{0:T(1024)}, u32[]{:S(2)}) copy-start(f32[1024]{0:T(1024)} %param.26) | copy-start | bytes 12292
  324.6 130.8 %copy-start.72 = (f32[256,4,4]{0,2,1:T(4,128)}, f32[256,4,4]{0,2,1:T(4,128)S(1)}, u32[]{:S(2)}) copy-start(f32[256,4,4]{0,2,1:T(4,128)S(1)} %copy.383) | copy-start | bytes 49156
  335.4 25.7 %copy-start.105 = (f32[256]{0:T(256)}, f32[256]{0:T(256)S(1)}, u32[]{:S(2)}) copy-start(f32[256]{0:T(256)S(1)} %fusion.74) | copy-start | bytes 3076
  335.4 25.7 %copy-start.95 = (f32[256]{0:T(256)}, f32[256]{0:T(256)S(1)}, u32[]{:S(2)}) copy-start(f32[256]{0:T(256)S(1)} %fusion.95) | copy-start | bytes 3076
  369.8 31.6 %copy-start.34 = (bf16[256,3072]{1,0:T(8,128)(2,1)}, bf16[256,3072]{1,0:T(8,128)(2,1)S(1)}, u32[]{:S(2)}) copy-start(bf16[256,3072]{1,0:T(8,128)(2,1)S(1)} %get-tuple-element.185) | copy-start | bytes 4718596
  417.2 9.4 copy-start.42
  426.5 5.8 copy-start.54
  426.5 5.8 copy-start.52
  432.4 6.1 copy-start
  438.4 16.9 %copy-start.68 = (f32[1,6,1024]{2,0,1:T(1,128)S(1)}, f32[1,6,1024]{2,0,1:T(1,128)}, u32[]{:S(2)}) copy-start(f32[1,6,1024]{2,0,1:T(1,128)} %get-tuple-element.165) | copy-start | bytes 73732
  438.4 16.9 %copy-start.70 = (f32[256,4,6]{0,2,1:T(8,128)S(1)}, f32[256,4,6]{0,2,1:T(8,128)}, u32[]{:S(2)}) copy-start(f32[256,4,6]{0,2,1:T(8,128)} %get-tuple-element.184) | copy-start | bytes 73732
  455.1 8.6 copy-start.88
  455.3 8.4 copy-start.86
  464.0 20.4 %copy-start.115 = (bf16[2048,1024]{1,0:T(8,128)(2,1)S(1)}, bf16[2048,1024]{1,0:T(8,128)(2,1)}, u32[]{:S(2)}) copy-start(bf16[2048,1024]{1,0:T(8,128)(2,1)} %all-gather.16.cloned.1.call-done) | copy-start | bytes 12582916
  510.4 11.8 %copy-start.29 = (bf16[128,2,8,2,128]{0,4,3,2,1:T(8,128)(2,1)S(1)}, bf16[128,2,8,2,128]{0,4,3,2,1:T(8,128)(2,1)}, u32[]{:S(2)}) copy-start(bf16[128,2,8,2,128]{0,4,3,2,1:T(8,128)(2,1)} %copy-done.28) | copy-start | bytes 3145732
  574.0 322.7 %reduce-scatter.6.cloned.1.call-start = ((), (), s32[]{:S(2)}) async-start(), calls=%async_computation.9 | async-start | bytes 33423360 | tf_op jit(solution)/shard_map/reduce_scatter | solution.py:304
  597.7 7.3 copy-start.35
  597.7 7.3 copy-start.43
  609.5 10.6 %copy-start.53 = (bf16[256,3072]{1,0:T(8,128)(2,1)S(1)}, bf16[256,3072]{1,0:T(8,128)(2,1)}, u32[]{:S(2)}) copy-start(bf16[256,3072]{1,0:T(8,128)(2,1)} %copy-done.52) | copy-start | bytes 4718596
  628.3 65.5 %copy-start.39 = (f32[256,128]{1,0:T(8,128)S(1)}, f32[256,128]{1,0:T(8,128)}, u32[]{:S(2)}) copy-start(f32[256,128]{1,0:T(8,128)} %copy-done.38) | copy-start | bytes 393220
  699.1 7.4 copy-start.16
  726.4 266.2 %all-reduce.13.cloned.1.call-start = ((), (), s32[]{:S(2)}) async-start(), calls=%async_computation.10 | async-start | bytes 3932160 | tf_op jit(solution)/shard_map/psum | solution.py:318
  732.4 11.7 %copy-start.81 = (f32[256,4]{1,0:T(8,128)S(1)}, f32[256,4]{1,0:T(8,128)}, u32[]{:S(2)}) copy-start(f32[256,4]{1,0:T(8,128)} %get-tuple-element.120) | copy-start | bytes 12292
  732.4 11.8 %copy-start.25 = (f32[256,1024]{1,0:T(8,128)S(1)}, f32[256,1024]{1,0:T(8,128)}, u32[]{:S(2)}) copy-start(f32[256,1024]{1,0:T(8,128)} %fusion.127) | copy-start | bytes 3145732
  732.4 11.8 %copy-start.51 = (f32[256,4,4]{2,1,0:T(4,128)S(1)}, f32[256,4,4]{2,1,0:T(4,128)}, u32[]{:S(2)}) copy-start(f32[256,4,4]{2,1,0:T(4,128)} %copy.375) | copy-start | bytes 49156
  732.4 11.8 %copy-start.56 = (f32[256,4,1]{1,0,2:T(8,128)S(1)}, f32[256,4,1]{1,0,2:T(8,128)}, u32[]{:S(2)}) copy-start(f32[256,4,1]{1,0,2:T(8,128)} %copy-done.55) | copy-start | bytes 12292
  744.2 14.3 %copy-start.73 = (f32[256,4,4]{0,2,1:T(4,128)S(1)}, f32[256,4,4]{0,2,1:T(4,128)}, u32[]{:S(2)}) copy-start(f32[256,4,4]{0,2,1:T(4,128)} %copy-done.72) | copy-start | bytes 49156
  744.2 14.3 %copy-start.87 = (f32[256,4,1]{0,2,1:T(1,128)S(1)}, f32[256,4,1]{0,2,1:T(1,128)}, u32[]{:S(2)}) copy-start(f32[256,4,1]{0,2,1:T(1,128)} %copy-done.86) | copy-start | bytes 12292
  744.2 14.3 %copy-start.89 = (f32[256,4,1]{0,2,1:T(1,128)S(1)}, f32[256,4,1]{0,2,1:T(1,128)}, u32[]{:S(2)}) copy-start(f32[256,4,1]{0,2,1:T(1,128)} %copy-done.88) | copy-start | bytes 12292
  744.2 14.4 %copy-start.7 = (f32[256,4,1024]{2,1,0:T(4,128)S(1)}, f32[256,4,1024]{2,1,0:T(4,128)}, u32[]{:S(2)}) copy-start(f32[256,4,1024]{2,1,0:T(4,128)} %copy-done.6) | copy-start | bytes 12582916
  744.2 14.4 %copy-start.71 = (f32[256,4,6]{0,2,1:T(8,128)S(1)}, f32[256,4,6]{0,2,1:T(8,128)}, u32[]{:S(2)}) copy-start(f32[256,4,6]{0,2,1:T(8,128)} %get-tuple-element.184) | copy-start | bytes 73732
  756.4 6.5 copy-start.27
  756.4 6.5 copy-start.114
  768.2 8.5 copy-start.66
  768.2 8.5 copy-start.69
  900.1 75.1 %copy-start.41 = (f32[256,4,4]{2,1,0:T(4,128)S(1)}, f32[256,4,4]{2,1,0:T(4,128)}, u32[]{:S(2)}) copy-start(f32[256,4,4]{2,1,0:T(4,128)} %copy-done.40) | copy-start | bytes 49156
  900.1 75.1 %copy-start.59 = (f32[256,4,1]{1,0,2:T(8,128)S(1)}, f32[256,4,1]{1,0,2:T(8,128)}, u32[]{:S(2)}) copy-start(f32[256,4,1]{1,0,2:T(8,128)} %copy-done.58) | copy-start | bytes 12292
  (64 other events, 166.8 us)
Sparse Core Ops, SparseCore 0:
  9.7 36.5 all-gather.7
  48.0 34.1 all-gather.9
  83.9 37.3 all-gather.13
  123.9 120.8 all-gather.11
  246.3 36.1 all-gather.15
  284.6 71.8 all-gather.17
  358.2 43.1 all-gather.19
  574.1 115.3 reduce-scatter.7
  726.5 170.2 reduce-scatter.5
  899.1 92.0 all-reduce.12
where the time goes:
time: 1020 us; the launch traced here: 1010 us
  waiting for transfers between devices  404 us (40%)
  matrix products  284 us (28%)
  local copies, waits for them, and re-layouts  131 us (13%)
  other arithmetic  101 us (10%)
  blocking collectives  69.7 us (7%)
  between operations  16.2 us (2%)
    reduce_scatter x1, waiting for transfers between devices, on_device(): lax.psum_scatter(jnp.concatenate([attn_part[:, :qkv_edge], mlp_part[:, :g...  112 us
    all_gather x1, waiting for transfers between devices, on_device(): lax.all_gather(jnp.stack([key_local, value_local], axis=2), 'rep', axis=0...  109 us
    dot_general x6, matrix products, lane_outputs(): jnp.einsum('tij,tid->tjd', mix_coef, lanes, precision=lax.Precision.HIGHEST)  82.9 us
    psum x1, blocking collectives, on_device(): lax.psum((grad_attn_gain, grad_mlp_gain, grad_query_gain, grad_key_gain,...  69.7 us
    unnamed x11, waiting for transfers between devices  64.6 us
    dot_general x4, matrix products, lane_inputs(): jnp.einsum('ts,tsd->td', coeffs[:, :, 0], lanes, precision=lax.Precision....  40 us
    unnamed x243, local copies, waits for them, and re-layouts  36.2 us
    all_gather x1, waiting for transfers between devices, on_device(): lax.all_gather(w_down, 'shard', axis=0, tiled=True)  31.6 us
  transfers between devices with their start and end apart: 10, of which 9 were waited for; matrix products, arithmetic and copies ran while one was open for 28% of the time, Pallas kernels for 0%

commit v1 on v0

v1 whole, which is shorter than its diff:
```python
from functools import partial

import jax
import jax.numpy as jnp
from jax import lax
from jax.experimental import pallas as pl
from jax.experimental.pallas import tpu as pltpu
from jax.sharding import PartitionSpec as P

EPSILON = 1e-06
ROTARY_BASE = 1000000.0
MASKED = -1e30
LANES = 4
SPAN = 32
PACK = 128
NT = (((1,), (1,)), ((), ()))
NN = (((1,), (0,)), ((), ()))
TN = (((0,), (0,)), ((), ()))
F32 = jnp.float32
BF16 = jnp.bfloat16
VMEM_LIMIT = 60 * 1024 * 1024
CHUNK = 64


def mm(a, b, dims=NN):
    return lax.dot_general(a, b, dims, preferred_element_type=F32)


def params(limit=VMEM_LIMIT):
    return pltpu.CompilerParams(vmem_limit_bytes=limit)


def lane_mask(column):
    spot = lax.broadcasted_iota(jnp.int32, (1, PACK), 1)
    return (spot == column).astype(F32)


def group_mask(lane):
    spot = lax.broadcasted_iota(jnp.int32, (1, PACK), 1)
    return (spot // 8 == lane).astype(F32)


def row_sum(values):
    return jnp.sum(values, axis=1, keepdims=True)


def col(coefs, index):
    return coefs[:, index : index + 1]


def rsqrt_mean(values):
    return lax.rsqrt(row_sum(values * values) * (1.0 / values.shape[1]) + EPSILON)


def lanes_of(ref, rows, width):
    return [ref[rows, i * width : (i + 1) * width].astype(F32) for i in range(LANES)]


def scale_pack(lanes):
    out = 0.0
    for i, h in enumerate(lanes):
        out = out + rsqrt_mean(h) * group_mask(i)
    return out


def mixed(coefs, lanes, j):
    out = col(coefs, 1 + j) * lanes[0]
    for i in range(1, LANES):
        out = out + col(coefs, 8 * i + 1 + j) * lanes[i]
    return out


def unmixed(coefs, grads, i):
    out = col(coefs, 8 * i + 1) * grads[0]
    for j in range(1, LANES):
        out = out + col(coefs, 8 * i + 1 + j) * grads[j]
    return out


def joined(coefs, lanes):
    out = col(coefs, 0) * lanes[0]
    for i in range(1, LANES):
        out = out + col(coefs, 8 * i) * lanes[i]
    return out


def branch_grad(coefs, grads):
    out = col(coefs, 5) * grads[0]
    for j in range(1, LANES):
        out = out + col(coefs, 8 * j + 5) * grads[j]
    return out


def mix_grads(lanes, grads, branch):
    out = 0.0
    for j in range(LANES):
        for i in range(LANES):
            out = out + row_sum(lanes[i] * grads[j]) * lane_mask(8 * i + 1 + j)
        out = out + row_sum(branch * grads[j]) * lane_mask(8 * j + 5)
    return out


def fold_low(raw):
    return raw + (pltpu.roll(raw, PACK - 2 * SPAN, 1) + pltpu.roll(raw, PACK - 3 * SPAN, 1))


def two_parts(values):
    high = values.astype(BF16)
    return high, (values - high.astype(F32)).astype(BF16)


def split_pack(values):
    high = values.astype(BF16).astype(F32)
    return (high + pltpu.roll(values - high, SPAN, 1) + pltpu.roll(high, 2 * SPAN, 1)).astype(BF16)


def hyper_rows(dtr_pack, lane_low, i):
    full = mm(dtr_pack, lane_low, TN)
    return full[8 * i : 8 * i + 8] + full[SPAN + 8 * i : SPAN + 8 * i + 8]


def fold8(values):
    rows = values.shape[0]
    out = values[0:8]
    for at in range(8, rows, 8):
        out = out + values[at : at + 8]
    return out


def pack_kernel(w_ref, out_ref):
    layers, count, width = w_ref.shape
    blank = jnp.zeros((8, width), F32)
    for layer in range(layers):
        w = jnp.concatenate([w_ref[layer], jnp.zeros((8 - count, width), F32)], axis=0)
        high = w.astype(BF16).astype(F32)
        for i in range(LANES):
            pieces = [blank] * (PACK // 8)
            pieces[i] = pieces[SPAN // 8 + i] = high
            pieces[2 * SPAN // 8 + i] = low = (w - high).astype(BF16).astype(F32)
            pieces[3 * SPAN // 8 + i] = (w - high) - low
            out_ref[layer, i] = jnp.concatenate(pieces, axis=0).astype(BF16)


def pack(hyper_weight):
    layers, _, width = hyper_weight.shape
    vm = pl.BlockSpec(memory_space=pltpu.VMEM)
    return pl.pallas_call(
        pack_kernel,
        in_specs=[vm],
        out_specs=vm,
        out_shape=jax.ShapeDtypeStruct((layers, LANES, PACK, width), BF16),
        compiler_params=params(),
        name="pack_hyper_weights",
    )(hyper_weight)


def pre_kernel(h_ref, w_ref, static_ref, gain_ref, x_ref, coef_ref, z_ref, raw_ref):
    rows, width = x_ref.shape
    acc = 0.0
    for i in range(LANES):
        acc = acc + mm(h_ref[:, i * width : (i + 1) * width], w_ref[i], NT)
    raw_ref[...] = acc

    @pl.loop(0, rows // CHUNK)
    def _(step):
        rs = pl.ds(pl.multiple_of(step * CHUNK, CHUNK), CHUNK)
        lanes = lanes_of(h_ref, rs, width)
        z = fold_low(raw_ref[rs, :]) * scale_pack(lanes)
        coefs = jnp.tanh(z) + static_ref[...]
        x = joined(coefs, lanes)
        x_ref[rs, :] = (x * rsqrt_mean(x) * gain_ref[...]).astype(BF16)
        coef_ref[rs, :] = coefs
        z_ref[rs, :] = z


def pre(h, wrow, static, gain):
    rows, width4 = h.shape
    width = width4 // LANES
    block = rows // 2
    return pl.pallas_call(
        pre_kernel,
        grid=(2,),
        in_specs=[
            pl.BlockSpec((block, width4), lambda g: (g, 0)),
            pl.BlockSpec((LANES, PACK, width), lambda g: (0, 0, 0)),
            pl.BlockSpec((1, PACK), lambda g: (0, 0)),
            pl.BlockSpec((1, width), lambda g: (0, 0)),
        ],
        out_specs=[
            pl.BlockSpec((block, width), lambda g: (g, 0)),
            pl.BlockSpec((block, PACK), lambda g: (g, 0)),
            pl.BlockSpec((block, PACK), lambda g: (g, 0)),
        ],
        out_shape=[
            jax.ShapeDtypeStruct((rows, width), BF16),
            jax.ShapeDtypeStruct((rows, PACK), F32),
            jax.ShapeDtypeStruct((rows, PACK), F32),
        ],
        scratch_shapes=[pltpu.VMEM((block, PACK), F32)],
        compiler_params=params(),
        name="lane_in_zero",
    )(h, wrow, static, gain)


def rotate(u, gain, cos, sin_signed):
    half = u.shape[1] // 2
    m = u * rsqrt_mean(u) * gain
    return m * cos + pltpu.roll(m, half, 1) * sin_signed


def qkv_kernel(x_ref, w_ref, qg_ref, kg_ref, cos_ref, sin_ref, send_ref, keep_ref):
    hd = qg_ref.shape[1]
    rows = x_ref.shape[0]
    half = x_ref.shape[1] // 2
    u = 0.0
    for z in range(2):
        w = w_ref[:, z].reshape(half, 4 * hd)
        u = u + mm(x_ref[:, z * half : (z + 1) * half], w)
    half_rows = rows // 2
    for part in range(2):
        rs = slice(part * half_rows, (part + 1) * half_rows)
        cos, sin = cos_ref[...], sin_ref[...]
        for k in range(3):
            cs = slice(k * hd, (k + 1) * hd)
            piece = u[rs, cs]
            keep_ref[0, rs, cs] = piece
            gain = qg_ref[...] if k < 2 else kg_ref[...]
            send_ref[0, rs, cs] = rotate(piece, gain, cos, sin).astype(BF16)
        send_ref[0, rs, 3 * hd :] = u[rs, 3 * hd :].astype(BF16)


def qkv(x, w_grouped, q_gain, k_gain, cos, sin_signed):
    rows, width = x.shape
    hd = q_gain.shape[1]
    groups = w_grouped.shape[3] // (4 * hd)
    return pl.pallas_call(
        qkv_kernel,
        grid=(groups,),
        in_specs=[
            pl.BlockSpec((rows, width), lambda g: (0, 0)),
            pl.BlockSpec(w_grouped.shape[:3] + (4 * hd,), lambda g: (0, 0, 0, g)),
            pl.BlockSpec((1, hd), lambda g: (0, 0)),
            pl.BlockSpec((1, hd), lambda g: (0, 0)),
            pl.BlockSpec(cos.shape, lambda g: (0, 0)),
            pl.BlockSpec(cos.shape, lambda g: (0, 0)),
        ],
        out_specs=[
            pl.BlockSpec((1, rows, 4 * hd), lambda g: (g, 0, 0)),
            pl.BlockSpec((1, rows, 3 * hd), lambda g: (g, 0, 0)),
        ],
        out_shape=[
            jax.ShapeDtypeStruct((groups, rows, 4 * hd), BF16),
            jax.ShapeDtypeStruct((groups, rows, 3 * hd), F32),
        ],
        compiler_params=params(),
        name="qkv_rotary",
    )(x, w_grouped, q_gain, k_gain, cos, sin_signed)


QB = 256


def allowed_at(i, kb, length, block):
    row = lax.broadcasted_iota(jnp.int32, (2 * block, block), 0)
    row = jnp.where(row >= block, row - block, row) + i * block
    key = lax.broadcasted_iota(jnp.int32, (2 * block, block), 1) + kb * block
    return (key <= row) & (key < length)


def two_heads(ref, i, per, hd, at=0):
    first = ref[pl.ds(i * per, per), 0, :, at * hd : (at + 1) * hd]
    second = ref[pl.ds(i * per, per), 0, :, (at + 1) * hd : (at + 2) * hd]
    return jnp.concatenate([first.reshape(-1, hd), second.reshape(-1, hd)], axis=0)


def one_head(ref, i, per, hd, at):
    return ref[pl.ds(i * per, per), 0, :, at * hd : (at + 1) * hd].reshape(-1, hd)


def attend_kernel(len_ref, x_ref, o_ref, lse_ref, s_ref):
    sources, _, places, width = x_ref.shape
    hd = width // 4
    per = QB // places
    scale = hd**-0.5
    length = len_ref[pl.program_id(0)]

    @pl.loop(0, sources * places // QB)
    def _(i):
        q = two_heads(x_ref, i, per, hd)

        def score(kb, top):
            s = mm(q, one_head(x_ref, kb, per, hd, 2), NT) * scale
            s = jnp.where(allowed_at(i, kb, length, QB), s, MASKED)
            s_ref[kb] = s
            for at in range(0, QB, 128):
                top = jnp.maximum(top, s[:, at : at + 128])
            return top

        top = lax.fori_loop(0, i + 1, score, jnp.full((2 * QB, 128), MASKED, F32))
        top = jnp.max(top, axis=1, keepdims=True)

        def weigh(kb, total):
            p = jnp.exp(s_ref[kb] - top)
            s_ref[kb] = p
            for at in range(0, QB, 128):
                total = total + p[:, at : at + 128]
            return total

        total = row_sum(lax.fori_loop(0, i + 1, weigh, jnp.zeros((2 * QB, 128), F32)))
        inverse = 1.0 / total

        def gather(kb, acc):
            p = (s_ref[kb] * inverse).astype(BF16)
            return acc + mm(p, one_head(x_ref, kb, per, hd, 3))

        o = lax.fori_loop(0, i + 1, gather, jnp.zeros((2 * QB, hd), F32)).astype(BF16)
        lse_ref[0, i] = jnp.broadcast_to(top + jnp.log(total), (2 * QB, 128))
        o_ref[pl.ds(i * per, per), 0, :, 0:hd] = o[:QB].reshape(per, places, hd)
        o_ref[pl.ds(i * per, per), 0, :, hd:] = o[QB:].reshape(per, places, hd)


def attend(lengths, x):
    sources, pairs, places, width = x.shape
    hd = width // 4
    blocks = sources * places // QB
    return pl.pallas_call(
        attend_kernel,
        grid=(pairs,),
        in_specs=[
            pl.BlockSpec(memory_space=pltpu.SMEM),
            pl.BlockSpec((sources, 1, places, width), lambda b: (0, b, 0, 0)),
        ],
        out_specs=[
            pl.BlockSpec((sources, 1, places, 2 * hd), lambda b: (0, b, 0, 0)),
            pl.BlockSpec((1, blocks, 2 * QB, 128), lambda b: (b, 0, 0, 0)),
        ],
        out_shape=[
            jax.ShapeDtypeStruct((sources, pairs, places, 2 * hd), BF16),
            jax.ShapeDtypeStruct((pairs, blocks, 2 * QB, 128), F32),
        ],
        scratch_shapes=[pltpu.VMEM((blocks, 2 * QB, QB), F32)],
        compiler_params=params(),
        name="attend",
    )(lengths, x)


def attend_back_kernel(
    len_ref, x_ref, do_ref, lse_ref, out_ref, dk_ref, dv_ref, p_ref, dp_ref
):
    sources, _, places, width = x_ref.shape
    hd = width // 4
    per = QB // places
    scale = hd**-0.5
    length = len_ref[pl.program_id(0)]
    blocks = sources * places // QB
    dk_ref[...] = jnp.zeros_like(dk_ref)
    dv_ref[...] = jnp.zeros_like(dv_ref)

    @pl.loop(0, blocks)
    def _(i):
        q = two_heads(x_ref, i, per, hd)
        do = two_heads(do_ref, i, per, hd)
        lse = lse_ref[0, i][:, 0:1]

        def weigh(kb, carry):
            total, delta = carry
            s = mm(q, one_head(x_ref, kb, per, hd, 2), NT) * scale
            p = jnp.where(allowed_at(i, kb, length, QB), jnp.exp(s - lse), 0.0)
            dp = mm(do, one_head(x_ref, kb, per, hd, 3), NT)
            p_ref[kb] = p
            dp_ref[kb] = dp
            pdp = p * dp
            for at in range(0, QB, 128):
                total = total + p[:, at : at + 128]
                delta = delta + pdp[:, at : at + 128]
            dv_ref[kb] += mm(p.astype(BF16), do, TN)
            return total, delta

        zero = jnp.zeros((2 * QB, 128), F32)
        total, delta = lax.fori_loop(0, i + 1, weigh, (zero, zero))
        delta = row_sum(delta) / row_sum(total)

        def spread(kb, dq):
            ds = (p_ref[kb] * (dp_ref[kb] - delta)).astype(BF16)
            dk_ref[kb] += mm(ds, q, TN)
            return dq + mm(ds, one_head(x_ref, kb, per, hd, 2))

        dq = lax.fori_loop(0, i + 1, spread, jnp.zeros((2 * QB, hd), F32))
        dq = (dq * scale).astype(BF16)
        out_ref[pl.ds(i * per, per), 0, :, 0:hd] = dq[:QB].reshape(per, places, hd)
        out_ref[pl.ds(i * per, per), 0, :, hd : 2 * hd] = dq[QB:].reshape(per, places, hd)

    @pl.loop(0, blocks)
    def _(i):
        dk = (dk_ref[i] * scale).astype(BF16)
        out_ref[pl.ds(i * per, per), 0, :, 2 * hd : 3 * hd] = dk.reshape(per, places, hd)
        out_ref[pl.ds(i * per, per), 0, :, 3 * hd :] = (
            dv_ref[i].astype(BF16).reshape(per, places, hd)
        )


def attend_back(lengths, x, do, lse):
    sources, pairs, places, width = x.shape
    hd = width // 4
    blocks = sources * places // QB
    return pl.pallas_call(
        attend_back_kernel,
        grid=(pairs,),
        in_specs=[
            pl.BlockSpec(memory_space=pltpu.SMEM),
            pl.BlockSpec((sources, 1, places, width), lambda b: (0, b, 0, 0)),
            pl.BlockSpec((sources, 1, places, 2 * hd), lambda b: (0, b, 0, 0)),
            pl.BlockSpec((1, blocks, 2 * QB, 128), lambda b: (b, 0, 0, 0)),
        ],
        out_specs=pl.BlockSpec((sources, 1, places, width), lambda b: (0, b, 0, 0)),
        out_shape=jax.ShapeDtypeStruct((sources, pairs, places, width), BF16),
        scratch_shapes=[
            pltpu.VMEM((blocks, QB, hd), F32),
            pltpu.VMEM((blocks, QB, hd), F32),
            pltpu.VMEM((blocks, 2 * QB, QB), F32),
            pltpu.VMEM((blocks, 2 * QB, QB), F32),
        ],
        compiler_params=params(),
        name="attend_back",
    )(lengths, x, do, lse)


def lane_in_back_one(lanes, coefs, static, dxn, gain, dcoef):
    x = joined(coefs, lanes)
    r = rsqrt_mean(x)
    xr = x * r
    dgain = dxn * xr
    e = dxn * gain
    dx = r * (e - xr * (row_sum(e * xr) * (1.0 / x.shape[1])))
    for i in range(LANES):
        dcoef = dcoef + row_sum(lanes[i] * dx) * lane_mask(8 * i)
    t = coefs - static
    return dx, dgain, dcoef, dcoef * (1.0 - t * t)


def lane_in_back_two(lane, alpha, dx, dhn, r, mean):
    return alpha * dx + r * (dhn - lane * (r * mean))


def group_mean(values, lane, width):
    return row_sum(values * group_mask(lane)) * (1.0 / width)


def middle_kernel(
    info_ref,
    h_ref,
    cot_ref,
    o_ref,
    ca_ref,
    wrow_ref,
    static_ref,
    gain_ref,
    weights_ref,
    out_ref,
    dh_ref,
    dca_ref,
    do_ref,
    xb_ref,
    dgu_ref,
    hid_ref,
    dyb_ref,
    dya_ref,
    dgain_ref,
    dhyper_ref,
    dstatic_ref,
    wo,
    wgu,
    wd,
    h1,
    ya,
    yb,
    gate,
    up,
    cb,
    zb,
    rb,
    raw,
    dcoef,
    sem,
):
    rows, width = xb_ref.shape
    groups = o_ref.shape[0]
    ff = hid_ref.shape[1]
    shards = wo.shape[0]
    out_rows, gu_rows, down_rows = wo.shape[1], wgu.shape[2], wd.shape[1]
    tiles = wgu.shape[0]
    half_tiles = tiles // 2
    chunks = rows // CHUNK

    def load(start, count, where, index):
        half = shards // 2
        return [
            pltpu.make_async_copy(
                weights_ref.at[:, z, pl.ds(start, count), :],
                where.at[pl.ds(z * half, half)],
                sem.at[2 * index + z],
            )
            for z in range(2)
        ]

    copies = [load(0, out_rows, wo, 0)]
    for t in range(tiles):
        copies.append(load(out_rows + t * gu_rows, gu_rows, wgu.at[t], 1 + t))
    copies.append(load(out_rows + tiles * gu_rows, down_rows, wd, 1 + tiles))
    for pair in copies:
        for copy in pair:
            copy.start()

    def arrive(pairs):
        for pair in pairs:
            for copy in pair:
                copy.wait()

    def chunk(step):
        return pl.ds(pl.multiple_of(step * CHUNK, CHUNK), CHUNK)

    tile = 256

    def tile_at(n):
        return pl.ds(pl.multiple_of(n * tile, tile), tile)

    arrive(copies[:1])

    @pl.loop(0, width // tile)
    def _(n):
        acc = 0.0
        for j in range(groups):
            span = o_ref.shape[2]
            per = span // out_rows
            w = wo[j * per : (j + 1) * per, :, tile_at(n)].reshape(span, tile)
            acc = acc + mm(o_ref[j], w)
        ya[:, tile_at(n)] = acc

    @pl.loop(0, chunks)
    def _(step):
        rs = chunk(step)
        lanes = lanes_of(h_ref, rs, width)
        coefs = ca_ref[rs, :]
        branch = ya[rs, :]
        new = []
        for j in range(LANES):
            new.append(mixed(coefs, lanes, j) + col(coefs, 8 * j + 5) * branch)
            h1[rs, j * width : (j + 1) * width] = new[j]
        rb[rs, :] = scale_pack(new)

    acc = 0.0
    for i in range(LANES):
        cs = slice(i * width, (i + 1) * width)
        for piece in two_parts(h1[:, cs]):
            acc = acc + mm(piece, wrow_ref[i], NT)
    raw[...] = acc

    @pl.loop(0, chunks)
    def _(step):
        rs = chunk(step)
        z = fold_low(raw[rs, :]) * rb[rs, :]
        coefs = jnp.tanh(z) + static_ref[...]
        cb[rs, :] = coefs
        zb[rs, :] = z
        x = joined(coefs, lanes_of(h1, rs, width))
        xb_ref[rs, :] = (x * rsqrt_mean(x) * gain_ref[...]).astype(BF16)

    arrive(copies[1:-1])
    for t in range(half_tiles):

        @pl.loop(0, width // tile)
        def _(n):
            x = xb_ref[...]
            cs = pl.ds(pl.multiple_of(t * width + n * tile, tile), tile)
            g = mm(x, wgu[t, :, :, tile_at(n)].reshape(width, tile))
            u = mm(x, wgu[half_tiles + t, :, :, tile_at(n)].reshape(width, tile))
            gate[:, cs] = g
            up[:, cs] = u
            hid_ref[:, cs] = (g / (1.0 + jnp.exp(-g)) * u).astype(BF16)

    arrive(copies[-1:])

    @pl.loop(0, width // tile)
    def _(n):
        yb[:, tile_at(n)] = mm(hid_ref[...], wd[:, :, tile_at(n)].reshape(ff, tile))

    @pl.loop(0, chunks)
    def _(step):
        rs = chunk(step)
        per_pair = rows // 2
        pair = step * CHUNK // per_pair
        place = info_ref[2] + lax.rem(step * CHUNK, per_pair)
        spot = place + lax.broadcasted_iota(jnp.int32, (CHUNK, 1), 0)
        valid = (spot < info_ref[pair]).astype(F32)
        lanes = lanes_of(h1, rs, width)
        coefs = cb[rs, :]
        branch = yb[rs, :]
        for j in range(LANES):
            new = mixed(coefs, lanes, j) + col(coefs, 8 * j + 5) * branch
            out_ref[rs, j * width : (j + 1) * width] = new.astype(BF16)
        grads = [g * valid for g in lanes_of(cot_ref, rs, width)]
        dcoef[rs, :] = mix_grads(lanes, grads, branch)
        dyb_ref[rs, :] = branch_grad(coefs, grads).astype(BF16)

    step_ff = 2 * down_rows

    @pl.loop(0, ff // step_ff)
    def _(s):
        cs = pl.ds(pl.multiple_of(s * step_ff, 128), step_ff)
        dhid = mm(dyb_ref[...], wd[pl.ds(2 * s, 2)].reshape(step_ff, width), NT)
        g = gate[:, cs]
        z = 1.0 / (1.0 + jnp.exp(-g))
        gz = g * z
        dgu_ref[:, cs] = (dhid * up[:, cs] * (z + gz * (1.0 - z))).astype(BF16)
        cs_up = pl.ds(pl.multiple_of(ff + s * step_ff, 128), step_ff)
        dgu_ref[:, cs_up] = (dhid * gz).astype(BF16)

    per = tile // gu_rows

    @pl.loop(0, width // tile)
    def _(n):
        acc = 0.0
        for t in range(tiles):
            w = wgu[t, pl.ds(n * per, per)].reshape(tile, width)
            acc = acc + mm(dgu_ref[:, t * width : (t + 1) * width], w, NT)
        yb[:, tile_at(n)] = acc

    dgain_ref[...] = jnp.zeros_like(dgain_ref)
    dstatic_ref[...] = jnp.zeros_like(dstatic_ref)

    @pl.loop(0, chunks)
    def _(step):
        rs = chunk(step)
        lanes = lanes_of(h1, rs, width)
        dx, dgain, dc, dt = lane_in_back_one(
            lanes, cb[rs, :], static_ref[...], yb[rs, :], gain_ref[...], dcoef[rs, :]
        )
        yb[rs, :] = dx
        dgain_ref[...] += fold8(dgain)
        dstatic_ref[...] += fold8(dc)
        dcoef[rs, :] = dt

    dt_low = split_pack(dcoef[...])
    dtr_low = split_pack(dcoef[...] * rb[...])
    dh_scr = gate
    for i in range(LANES):
        cs = slice(i * width, (i + 1) * width)
        part = hyper_rows(dtr_low, h1[:, cs].astype(BF16), i)
        if i == 0:
            dhyper_ref[...] = part
        else:
            dhyper_ref[...] += part
        dhn = mm(dt_low, wrow_ref[i])
        if i < LANES - 1:
            dh_scr[:, cs] = dhn
        else:
            up[:, 0:width] = dhn

    @pl.loop(0, chunks)
    def _(step):
        rs = chunk(step)
        per_pair = rows // 2
        pair = step * CHUNK // per_pair
        place = info_ref[2] + lax.rem(step * CHUNK, per_pair)
        spot = place + lax.broadcasted_iota(jnp.int32, (CHUNK, 1), 0)
        valid = (spot < info_ref[pair]).astype(F32)
        lanes = lanes_of(h1, rs, width)
        cots = [g * valid for g in lanes_of(cot_ref, rs, width)]
        coefs = cb[rs, :]
        dx = yb[rs, :]
        dtz = dcoef[rs, :] * zb[rs, :]
        scales = rb[rs, :]
        grads = []
        for i in range(LANES):
            if i < LANES - 1:
                dhn = dh_scr[rs, i * width : (i + 1) * width]
            else:
                dhn = up[rs, 0:width]
            back = lane_in_back_two(
                lanes[i], col(coefs, 8 * i), dx, dhn, col(scales, 8 * i), group_mean(dtz, i, width)
            )
            grads.append(unmixed(coefs, cots, i) + back)
        zero = lanes_of(h_ref, rs, width)
        coefs_a = ca_ref[rs, :]
        dca_ref[rs, :] = mix_grads(zero, grads, ya[rs, :])
        dya_ref[rs, :] = branch_grad(coefs_a, grads).astype(BF16)
        for i in range(LANES):
            dh_ref[rs, i * width : (i + 1) * width] = unmixed(coefs_a, grads, i)

    @pl.loop(0, groups)
    def _(j):
        span = o_ref.shape[2]
        per = span // out_rows
        w = wo[pl.ds(j * per, per)].reshape(span, width)
        do_ref[j] = mm(dya_ref[...], w, NT).astype(BF16)


def middle(info, h, cot, o, ca, wrow, static, gain, weights, out_rows, gu_rows, down_rows):
    rows, width4 = h.shape
    width = width4 // LANES
    shards = weights.shape[0] * weights.shape[1]
    ff = shards * down_rows
    tiles = 2 * ff // width
    groups, _, span = o.shape
    vm = pl.BlockSpec(memory_space=pltpu.VMEM)
    sds = jax.ShapeDtypeStruct
    return pl.pallas_call(
        middle_kernel,
        in_specs=[pl.BlockSpec(memory_space=pltpu.SMEM)]
        + [vm] * 7
        + [pl.BlockSpec(memory_space=pl.ANY)],
        out_specs=[vm] * 12,
        out_shape=[
            sds((rows, width4), BF16),
            sds((rows, width4), F32),
            sds((rows, PACK), F32),
            sds((groups, rows, span), BF16),
            sds((rows, width), BF16),
            sds((rows, 2 * ff), BF16),
            sds((rows, ff), BF16),
            sds((rows, width), BF16),
            sds((rows, width), BF16),
            sds((8, width), F32),
            sds((8, width), F32),
            sds((8, PACK), F32),
        ],
        scratch_shapes=[
            pltpu.VMEM((shards, out_rows, width), BF16),
            pltpu.VMEM((tiles, shards, gu_rows, width), BF16),
            pltpu.VMEM((shards, down_rows, width), BF16),
            pltpu.VMEM((rows, width4), F32),
            pltpu.VMEM((rows, width), F32),
            pltpu.VMEM((rows, width), F32),
            pltpu.VMEM((rows, ff), F32),
            pltpu.VMEM((rows, ff), F32),
            pltpu.VMEM((rows, PACK), F32),
            pltpu.VMEM((rows, PACK), F32),
            pltpu.VMEM((rows, PACK), F32),
            pltpu.VMEM((rows, PACK), F32),
            pltpu.VMEM((rows, PACK), F32),
            pltpu.SemaphoreType.DMA((2 * tiles + 4,)),
        ],
        compiler_params=params(),
        name="token_local",
    )(info, h, cot, o, ca, wrow, static, gain, weights)


def turn_back_kernel(
    d_ref, u_ref, x_ref, qg_ref, kg_ref, cos_ref, sin_ref, dqkv_ref, grad_ref, dqg_ref, dkg_ref
):
    hd = qg_ref.shape[1]
    rows = x_ref.shape[0]
    half_rows = rows // 2

    @pl.when(pl.program_id(0) == 0)
    def _():
        dqg_ref[...] = jnp.zeros_like(dqg_ref)
        dkg_ref[...] = jnp.zeros_like(dkg_ref)

    for part in range(2):
        rs = slice(part * half_rows, (part + 1) * half_rows)
        cos, sin = cos_ref[...], sin_ref[...]
        for k in range(3):
            cs = slice(k * hd, (k + 1) * hd)
            u = u_ref[0, rs, cs]
            dr = d_ref[0, rs, cs].astype(F32)
            dm = dr * cos - pltpu.roll(dr, hd // 2, 1) * sin
            r = rsqrt_mean(u)
            ur = u * r
            gain = qg_ref[...] if k < 2 else kg_ref[...]
            total = dqg_ref if k < 2 else dkg_ref
            total[...] += fold8(dm * ur)
            e = dm * gain
            du = r * (e - ur * (row_sum(e * ur) * (1.0 / hd)))
            dqkv_ref[0, rs, cs] = du.astype(BF16)
        dqkv_ref[0, rs, 3 * hd :] = d_ref[0, rs, 3 * hd :]
    half = x_ref.shape[1] // 2
    for z in range(2):
        grad = mm(x_ref[:, z * half : (z + 1) * half], dqkv_ref[0], TN)
        grad_ref[:, z] = grad.astype(BF16).reshape(grad_ref.shape[0], grad_ref.shape[2], 4 * hd)


def turn_back(d, u, x, q_gain, k_gain, cos, sin, shards):
    groups, rows, width4h = d.shape
    hd = width4h // 4
    width = x.shape[1]
    sds = jax.ShapeDtypeStruct

    def whole(a):
        return pl.BlockSpec(a.shape, lambda g: (0,) * a.ndim)

    return pl.pallas_call(
        turn_back_kernel,
        grid=(groups,),
        in_specs=[
            pl.BlockSpec((1, rows, 4 * hd), lambda g: (g, 0, 0)),
            pl.BlockSpec((1, rows, 3 * hd), lambda g: (g, 0, 0)),
        ]
        + [whole(a) for a in (x, q_gain, k_gain, cos, sin)],
        out_specs=[
            pl.BlockSpec((1, rows, 4 * hd), lambda g: (g, 0, 0)),
            pl.BlockSpec((shards // 2, 2, width // shards, 4 * hd), lambda g: (0, 0, 0, g)),
            pl.BlockSpec((8, hd), lambda g: (0, 0)),
            pl.BlockSpec((8, hd), lambda g: (0, 0)),
        ],
        out_shape=[
            sds((groups, rows, 4 * hd), BF16),
            sds((shards // 2, 2, width // shards, groups * 4 * hd), BF16),
            sds((8, hd), F32),
            sds((8, hd), F32),
        ],
        compiler_params=params(),
        name="rotary_back",
    )(d, u, x, q_gain, k_gain, cos, sin)


def last_kernel(
    dqkv_ref,
    w_ref,
    h_ref,
    c_ref,
    z_ref,
    dc_ref,
    dh_ref,
    wrow_ref,
    static_ref,
    gain_ref,
    dres_ref,
    dgain_ref,
    dhyper_ref,
    dstatic_ref,
    dx_ref,
    dt_ref,
    r_ref,
):
    groups, rows, span = dqkv_ref.shape
    width = gain_ref.shape[1]
    tile = 256

    per = tile // w_ref.shape[2]
    half_tiles = width // tile // 2

    @pl.loop(0, width // tile)
    def _(n):
        z, at = n // half_tiles, lax.rem(n, half_tiles) * per
        acc = 0.0
        for g in range(groups):
            w = w_ref[pl.ds(at, per), z, :, g * span : (g + 1) * span].reshape(tile, span)
            acc = acc + mm(dqkv_ref[g], w, NT)
        dx_ref[:, pl.ds(pl.multiple_of(n * tile, tile), tile)] = acc

    dgain_ref[...] = jnp.zeros_like(dgain_ref)
    dstatic_ref[...] = jnp.zeros_like(dstatic_ref)

    def chunk(step):
        return pl.ds(pl.multiple_of(step * CHUNK, CHUNK), CHUNK)

    @pl.loop(0, rows // CHUNK)
    def _(step):
        rs = chunk(step)
        lanes = lanes_of(h_ref, rs, width)
        dx, dgain, dc, dt = lane_in_back_one(
            lanes, c_ref[rs, :], static_ref[...], dx_ref[rs, :], gain_ref[...], dc_ref[rs, :]
        )
        dx_ref[rs, :] = dx
        dgain_ref[...] += fold8(dgain)
        dstatic_ref[...] += fold8(dc)
        dt_ref[rs, :] = dt
        r_ref[rs, :] = scale_pack(lanes)

    dt_low = split_pack(dt_ref[...])
    dtr_low = split_pack(dt_ref[...] * r_ref[...])
    for i in range(LANES):
        cs = slice(i * width, (i + 1) * width)
        part = hyper_rows(dtr_low, h_ref[:, cs], i)
        if i == 0:
            dhyper_ref[...] = part
        else:
            dhyper_ref[...] += part
        dres_ref[:, cs] = mm(dt_low, wrow_ref[i])

    @pl.loop(0, rows // CHUNK)
    def _(step):
        rs = chunk(step)
        coefs = c_ref[rs, :]
        dx = dx_ref[rs, :]
        dtz = dt_ref[rs, :] * z_ref[rs, :]
        scales = r_ref[rs, :]
        for i in range(LANES):
            cs = slice(i * width, (i + 1) * width)
            lane = h_ref[rs, cs].astype(F32)
            back = lane_in_back_two(
                lane,
                col(coefs, 8 * i),
                dx,
                dres_ref[rs, cs],
                col(scales, 8 * i),
                group_mean(dtz, i, width),
            )
            dres_ref[rs, cs] = dh_ref[rs, cs] + back


def last(dqkv, w_grouped, h, c, z, dc, dh, wrow, static, gain):
    rows, width4 = h.shape
    width = width4 // LANES
    vm = pl.BlockSpec(memory_space=pltpu.VMEM)
    sds = jax.ShapeDtypeStruct
    return pl.pallas_call(
        last_kernel,
        in_specs=[vm] * 10,
        out_specs=[vm] * 4,
        out_shape=[
            sds((rows, width4), F32),
            sds((8, width), F32),
            sds((8, width), F32),
            sds((8, PACK), F32),
        ],
        scratch_shapes=[
            pltpu.VMEM((rows, width), F32),
            pltpu.VMEM((rows, PACK), F32),
            pltpu.VMEM((rows, PACK), F32),
        ],
        compiler_params=params(),
        name="lane_in_back",
    )(dqkv, w_grouped, h, c, z, dc, dh, wrow, static, gain)


def grads_kernel(o_ref, dya_ref, xb_ref, dgu_ref, hid_ref, dyb_ref, out_ref):
    per, _, owned, width = out_ref.shape
    out_rows = o_ref.shape[0] * o_ref.shape[2] // per
    gu_rows = xb_ref.shape[1] // per
    down_rows = hid_ref.shape[1] // per
    tiles = dgu_ref.shape[1] // width
    piece = mm(hid_ref[...], dyb_ref[...], TN).astype(BF16)
    for s in range(per):
        at = out_rows + tiles * gu_rows
        out_ref[s, 0, at : at + down_rows, :] = piece[s * down_rows : (s + 1) * down_rows]
    for j in range(o_ref.shape[0]):
        piece = mm(o_ref[j], dya_ref[...], TN).astype(BF16)
        heads = o_ref.shape[2] // out_rows
        for s in range(heads):
            out_ref[j * heads + s, 0, 0:out_rows, :] = piece[s * out_rows : (s + 1) * out_rows]

    for t in range(tiles):
        cs = slice(t * width, (t + 1) * width)
        piece = mm(xb_ref[...], dgu_ref[:, cs], TN).astype(BF16)
        for s in range(per):
            at = out_rows + t * gu_rows
            out_ref[s, 0, at : at + gu_rows, :] = piece[s * gu_rows : (s + 1) * gu_rows]


def weight_grads(o, dya, xb, dgu, hid, dyb, shards):
    rows, width = xb.shape
    ff = hid.shape[1]
    groups, _, span = o.shape
    steps = 4
    per = shards // steps
    owned = (groups * span + 3 * ff) // shards
    return pl.pallas_call(
        grads_kernel,
        grid=(steps,),
        in_specs=[
            pl.BlockSpec((groups // steps, rows, span), lambda g: (g, 0, 0)),
            pl.BlockSpec((rows, width), lambda g: (0, 0)),
            pl.BlockSpec((rows, width // steps), lambda g: (0, g)),
            pl.BlockSpec((rows, 2 * ff), lambda g: (0, 0)),
            pl.BlockSpec((rows, ff // steps), lambda g: (0, g)),
            pl.BlockSpec((rows, width), lambda g: (0, 0)),
        ],
        out_specs=pl.BlockSpec((per, 1, owned, width), lambda g: (g % 2, g // 2, 0, 0)),
        out_shape=jax.ShapeDtypeStruct((shards // 2, 2, owned, width), BF16),
        compiler_params=params(),
        name="weight_grads",
    )(o, dya, xb, dgu, hid, dyb)


RING = 4


def pair_along(kind, count, stride):
    pairs = []
    for i in range(count):
        at = i // stride % RING
        to = at ^ 1 if kind == 0 else RING - 1 - at
        pairs.append((i, i + (to - at) * stride))
    return pairs


def swap_y(values, kind):
    return lax.ppermute(values, "rep", pair_along(kind, lax.axis_size("rep"), 1))


def swap_z(values, kind):
    rep, shard = lax.axis_size("rep"), lax.axis_size("shard")
    pairs = []
    for r in range(rep):
        for s in range(shard):
            z = 2 * (r // RING) + s // (shard // 2)
            to = z ^ 1 if kind == 0 else 3 - z
            target = (to // 2 * RING + r % RING) * shard + to % 2 * (shard // 2) + s % (shard // 2)
            pairs.append((r * shard + s, target))
    return lax.ppermute(values, ("rep", "shard"), pairs)


def z_place():
    return lax.axis_index("shard") // (lax.axis_size("shard") // 2)


def z_groups():
    half = lax.axis_size("shard") // 2
    return [list(range(half)), list(range(half, 2 * half))]


def gather_rows(block):
    mid = block.shape[1] // 2
    other = jnp.concatenate([swap_z(block[:, :mid], 0), swap_z(block[:, mid:], 1)], axis=1)
    first = z_place() == 0
    pair = jnp.stack([jnp.where(first, block, other), jnp.where(first, other, block)])
    return lax.all_gather(pair, "shard", axis_index_groups=z_groups())


def scatter_rows(parts):
    return lax.psum_scatter(
        parts, "shard", scatter_dimension=0, axis_index_groups=z_groups(), tiled=False
    )


def swap_xor(values, axis, stride):
    return lax.ppermute(values, axis, [(i, i ^ stride) for i in range(lax.axis_size(axis))])


def rep_sum(pair):
    first = z_place() == 0
    values = jnp.where(first, pair[0], pair[1])
    others = jnp.where(first, pair[1], pair[0])
    place = lax.axis_index("rep") % RING
    bits = [(place % 2 + place // 2) % 2, place // 2]
    mid = values.shape[1] // 2
    orders = ((0, 1), (1, 0))
    spans = (slice(0, mid), slice(mid, None))
    got = yield [(partial(swap_z, kind=o[0]), others[:, cs]) for o, cs in zip(orders, spans)]
    acc = [values[:, cs].astype(F32) + g.astype(F32) for cs, g in zip(spans, got)]
    half = values.shape[0]
    for step in range(2):
        half //= 2
        keep, give = [], []
        for o, a in zip(orders, acc):
            bit = bits[o[step]]
            keep.append(lax.dynamic_slice_in_dim(a, bit * half, half, 0))
            give.append(lax.dynamic_slice_in_dim(a, (1 - bit) * half, half, 0).astype(BF16))
        got = yield [(partial(swap_y, kind=o[step]), g) for o, g in zip(orders, give)]
        acc = [k + g.astype(F32) for k, g in zip(keep, got)]
    low = [a.astype(BF16) for a in acc]
    got = yield [(partial(swap_xor, axis="rep", stride=RING), v) for v in low]
    low = [(v.astype(F32) + g.astype(F32)).astype(BF16) for v, g in zip(low, got)]
    for step in (1, 0):
        got = yield [(partial(swap_y, kind=o[step]), v) for o, v in zip(orders, low)]
        for n, (o, g) in enumerate(zip(orders, got)):
            mine = bits[o[step]] == 0
            low[n] = jnp.concatenate(
                [jnp.where(mine, low[n], g), jnp.where(mine, g, low[n])], axis=0
            )
    return jnp.concatenate(low, axis=1)


def sum_everywhere(values):
    pairs = partial(pair_along, count=lax.axis_size("shard"), stride=2)
    swaps = [partial(swap_y, kind=0), partial(swap_y, kind=1)]
    swaps += [partial(swap_xor, axis="rep", stride=RING), partial(swap_xor, axis="shard", stride=1)]
    swaps += [lambda v, k=k: lax.ppermute(v, "shard", pairs(k)) for k in (0, 1)]
    swaps += [partial(swap_xor, axis="shard", stride=2 * RING)]
    for swap in swaps:
        (got,) = yield [(swap, values)]
        values = values + got
    return values


def rounds(*chains):
    results = [None] * len(chains)
    asked = {n: next(chain) for n, chain in enumerate(chains)}
    while asked:
        got = {n: [swap(value) for swap, value in wants] for n, wants in asked.items()}
        got = lax.optimization_barrier(got)
        asked = {}
        for n, values in got.items():
            try:
                asked[n] = chains[n].send(values)
            except StopIteration as end:
                results[n] = end.value
    return results


def rotary_tables(first, count, head_dim):
    half_dim = head_dim // 2
    inverse = ROTARY_BASE ** (-jnp.arange(half_dim, dtype=F32) * 2.0 / head_dim)
    places = (first + jnp.arange(count, dtype=jnp.int32)).astype(F32)
    angles = places[:, None] * inverse[None, :]
    cos, sin = jnp.cos(angles), jnp.sin(angles)
    return jnp.concatenate([cos, cos], axis=1), jnp.concatenate([-sin, sin], axis=1)


def packed_static(static):
    lanes, count = static.shape
    flat = jnp.pad(static, ((0, 0), (0, 8 - count))).reshape(1, lanes * 8)
    return jnp.pad(flat, ((0, 0), (0, PACK - lanes * 8)))


def on_device(
    residuals,
    lengths,
    w_query,
    w_key,
    w_value,
    w_out,
    w_gate,
    w_up,
    w_down,
    attn_gain,
    mlp_gain,
    query_gain,
    key_gain,
    hyper_weight,
    hyper_static,
    cotangent,
):
    pairs, places, lane_count, width = residuals.shape
    rows = pairs * places
    hd = query_gain.shape[0]
    rep = lax.axis_size("rep")
    shards = lax.axis_size("shard")
    local = w_query.shape[0]
    groups = w_key.shape[1] // hd
    ff = w_gate.shape[1]
    tiles = ff // width
    first = lax.axis_index("rep") * places

    grouped = jnp.concatenate(
        [
            w_query.reshape(local, groups, 2 * hd),
            w_key.reshape(local, groups, hd),
            w_value.reshape(local, groups, hd),
        ],
        axis=2,
    ).reshape(local, groups * 4 * hd)
    w_grouped = gather_rows(grouped)
    rest = jnp.concatenate(
        [w_out]
        + [w_gate[:, t * width : (t + 1) * width] for t in range(tiles)]
        + [w_up[:, t * width : (t + 1) * width] for t in range(tiles)]
        + [w_down],
        axis=0,
    )
    w_rest = gather_rows(rest)

    h = residuals.reshape(rows, lane_count * width)
    cot = cotangent.reshape(rows, lane_count * width)
    wrow = pack(hyper_weight)
    wrow_a, wrow_b = wrow[0], wrow[1]
    static_a, static_b = packed_static(hyper_static[0]), packed_static(hyper_static[1])
    gain_a, gain_b = attn_gain[None, :], mlp_gain[None, :]
    q_gain, k_gain = query_gain[None, :], key_gain[None, :]
    cos, sin = rotary_tables(first, places, hd)
    info = jnp.concatenate([lengths, first[None].astype(jnp.int32)])

    xa, ca, za = pre(h, wrow_a, static_a, gain_a)
    send, keep = qkv(xa, w_grouped, q_gain, k_gain, cos, sin)
    x = lax.all_to_all(send, "rep", 0, 0, tiled=True).reshape(rep, pairs, places, 4 * hd)
    o_own, lse = attend(lengths, x)
    o = lax.all_to_all(o_own.reshape(rep, rows, 2 * hd), "rep", 0, 0, tiled=True)
    (out, dh, dca, do, xb, dgu, hid, dyb, dya, dgain_b, dhyper_b, dstatic_b) = middle(
        info,
        h,
        cot,
        o,
        ca,
        wrow_b,
        static_b,
        gain_b,
        w_rest,
        w_out.shape[0],
        local,
        w_down.shape[0],
    )
    rest_part = weight_grads(o, dya, xb, dgu, hid, dyb, shards)
    do, rest_part = lax.optimization_barrier((do, rest_part))
    do_own = lax.all_to_all(do, "rep", 0, 0, tiled=True).reshape(rep, pairs, places, 2 * hd)
    rest_own = scatter_rows(rest_part)
    d_own = attend_back(lengths, x, do_own, lse)
    d = lax.all_to_all(d_own.reshape(rep, rows, 4 * hd), "rep", 0, 0, tiled=True)
    dqkv, qkv_part, dqg, dkg = turn_back(d, keep, xa, q_gain, k_gain, cos, sin, shards)
    dres, dgain_a, dhyper_a, dstatic_a = last(
        dqkv, w_grouped, h, ca, za, dca, dh, wrow_a, static_a, gain_a
    )
    count = hyper_weight.shape[1]
    small = jnp.concatenate(
        [
            dgain_a.sum(0),
            dgain_b.sum(0),
            dqg.sum(0),
            dkg.sum(0),
            dhyper_a[:count].reshape(-1),
            dhyper_b[:count].reshape(-1),
            dstatic_a.sum(0),
            dstatic_b.sum(0),
        ]
    ).reshape(-1, PACK)
    qkv_part, rest_own, dres, small = lax.optimization_barrier((qkv_part, rest_own, dres, small))
    qkv_own = scatter_rows(qkv_part)
    rest_low, small = rounds(rep_sum(rest_own), sum_everywhere(small))
    rest_sum = rest_low.astype(F32)
    at, edge = w_out.shape[0], w_out.shape[0] + 2 * tiles * local
    gu = rest_sum[at:edge].reshape(2, tiles, local, width).transpose(0, 2, 1, 3)
    gu = gu.reshape(2, local, ff)
    small = small.reshape(-1)
    (qkv_low,) = rounds(rep_sum(qkv_own))
    qkv_sum = qkv_low.astype(F32).reshape(local, groups, 4 * hd)
    sizes = [width, width, hd, hd, count * width, count * width, PACK, PACK]
    pieces, start = [], 0
    for size in sizes:
        pieces.append(small[start : start + size])
        start += size

    def unpack(flat):
        return flat[: 8 * lane_count].reshape(lane_count, 8)[:, :count]

    return (
        out.reshape(residuals.shape),
        dres.reshape(residuals.shape),
        qkv_sum[:, :, : 2 * hd].reshape(local, -1),
        qkv_sum[:, :, 2 * hd : 3 * hd].reshape(local, -1),
        qkv_sum[:, :, 3 * hd :].reshape(local, -1),
        rest_sum[:at],
        gu[0],
        gu[1],
        rest_sum[edge:],
        pieces[0],
        pieces[1],
        pieces[2],
        pieces[3],
        jnp.stack([pieces[4].reshape(count, width), pieces[5].reshape(count, width)]),
        jnp.stack([unpack(pieces[6]), unpack(pieces[7])]),
    )


def solution(mesh):
    lane_spec = P("shard", "rep", None, None)
    row_spec = P("shard", None)
    in_specs = (lane_spec, P("shard")) + (row_spec,) * 7 + (P(),) * 6 + (lane_spec,)
    out_specs = (lane_spec, lane_spec) + (row_spec,) * 7 + (P(),) * 6
    return jax.shard_map(
        on_device, mesh=mesh, in_specs=in_specs, out_specs=out_specs, check_vma=False
    )
```

time: 1020 us -> 526 us (0.52)
  matrix products: 284 us -> 0 us
  waiting for transfers between devices: 404 us -> 167 us
  Pallas kernels: 0 us -> 153 us
  local copies, waits for them, and re-layouts: 131 us -> 39.7 us
  other arithmetic: 101 us -> 22.8 us
  starting transfers between devices: 0.4 us -> 59.2 us
    dot_general x39 -> x0, matrix products: 273 us -> none  [the longest x6 82.9 us: lane_outputs(): jnp.einsum('tij,tid->tjd', mix_coef, lanes, precision=lax.Precision.HIGHEST)]
    all_gather x7 -> x2, waiting for transfers between devices: 228 us -> 41.4 us  [gather_rows(): return lax.all_gather(pair, 'shard', axis_index_groups=z_groups())]
    pallas_call x0 -> x9, Pallas kernels: none -> 153 us  [the longest x1 49.4 us: middle(): pl.pallas_call(middle_kernel, in_specs=[pl.BlockSpec(memory_space=pltpu.S...]
    reduce_scatter x1 -> x2, waiting for transfers between devices: 112 us -> 4.47 us  [scatter_rows(): lax.psum_scatter(parts, 'shard', scatter_dimension=0, axis_index_groups=z...]
    ppermute x0 -> x35, waiting for transfers between devices: none -> 78.6 us  [the longest x8 38.5 us: swap_z(): return lax.ppermute(values, ('rep', 'shard'), pairs)]
    psum x1 -> x0, blocking collectives: 69.7 us -> none  [on_device(): lax.psum((grad_attn_gain, grad_mlp_gain, grad_query_gain, grad_key_gain,...]
    unnamed x11 -> x4, waiting for transfers between devices: 64.6 us -> 0.07 us
    all_to_all x0 -> x2, blocking collectives: none -> 60.5 us  [the longest x1 35.8 us: on_device(): lax.all_to_all(send, 'rep', 0, 0, tiled=True)]
  transfers between devices with their start and end apart: 10 -> 41, of which waited for: 9 -> 30; matrix products, arithmetic and copies ran while one was open for 28% -> 9% of each run, Pallas kernels for 0% -> 18%
where the time goes in v1:
time: 526 us; the launch traced here: 517 us
  waiting for transfers between devices  167 us (32%)
  Pallas kernels  153 us (29%)
  blocking collectives  60.5 us (12%)
  starting transfers between devices  59.2 us (11%)
  local copies, waits for them, and re-layouts  39.7 us (8%)
  other arithmetic  22.8 us (4%)
  between operations  15 us (3%)
    pallas_call x1, Pallas kernels, middle(): pl.pallas_call(middle_kernel, in_specs=[pl.BlockSpec(memory_space=pltpu.S...  49.4 us
    all_gather x2, waiting for transfers between devices, gather_rows(): return lax.all_gather(pair, 'shard', axis_index_groups=z_groups())  41.4 us
    ppermute x8, waiting for transfers between devices, swap_z(): return lax.ppermute(values, ('rep', 'shard'), pairs)  38.5 us
    all_to_all x1, blocking collectives, on_device(): lax.all_to_all(send, 'rep', 0, 0, tiled=True)  35.8 us
    all_to_all x1, waiting for transfers between devices, on_device(): lax.all_to_all(d_own.reshape(rep, rows, 4 * hd), 'rep', 0, 0, tiled=True)  28.4 us
    pallas_call x1, Pallas kernels, attend_back(): pl.pallas_call(attend_back_kernel, grid=(pairs,), in_specs=[pl.BlockSpec(...  26.6 us
    ppermute x18, waiting for transfers between devices, swap_y(): lax.ppermute(values, 'rep', pair_along(kind, lax.axis_size('rep'), 1))  26 us
    all_to_all x1, blocking collectives, on_device(): lax.all_to_all(do, 'rep', 0, 0, tiled=True)  24.6 us
  transfers between devices with their start and end apart: 41, of which 30 were waited for; matrix products, arithmetic and copies ran while one was open for 9% of the time, Pallas kernels for 18%

profile of v1, /device:TPU:0, one launch (start us, length us, event | category | flops | bytes accessed | tf_op | source)
XLA Modules:
  0.0 517.4 jit_solution(14877638153414187115)
XLA Ops:
  10.4 2.1 collective-permute-start
  12.5 2.5 collective-permute-start.1
  15.3 3.5 collective-permute-done
  18.8 2.7 collective-permute-done.1
  24.8 2.3 collective-permute-start.3
  27.3 13.6 %collective-permute-done.2 = bf16[704,512]{1,0:T(8,128)(2,1)S(1)} collective-permute-done((bf16[704,512]{1,0:T(8,128)(2,1)S(1)}, bf16[704,512]{1,0:T(8,128)(2,1)S(1)}, u32[]{:S(2)}, u32[]{:S(2)}) %collective-permute-start.2) | collective-permute-done | bytes 720928 | tf_op jit(solution)/shard_map/ppermute | solution.py:1002
  40.9 1.8 collective-permute-done.3
  43.4 1.8 pad_maximum_fusion
  46.7 2.3 pack_hyper_weights.1
  49.0 3.9 copy.38
  53.6 1.6 slice_bitcast_fusion
  55.2 5.2 lane_in_zero.1
  61.4 12.1 %all-gather.5.cloned.1.call-done = bf16[16,64,4096]{2,1,0:T(8,128)(2,1)} async-done(((bf16[2,64,4096]{2,1,0:T(8,128)(2,1)}), bf16[16,64,4096]{2,1,0:T(8,128)(2,1)}) %all-gather.5.cloned.1.call-update) | async-done | bytes 8388624 | tf_op jit(solution)/shard_map/all_gather | solution.py:1019
  73.5 9.7 %qkv_rotary.1 = (bf16[8,256,512]{2,1,0:T(8,128)(2,1)}, f32[8,256,384]{2,1,0:T(8,128)}) custom-call(bf16[256,1024]{1,0:T(8,128)(2,1)} %get-tuple-element.78.x_ref, bf16[8,2,64,4096]{3,2,1,0:T(8,128)(2,1)} %bitcast.102, f32[1,128]{1,0:T(1,128)} %bitcast.147, f32[1,128]{1,0:T(1,128)} %bitcast.149, f32[128,128]{1,0:T(8,128)} %get-tuple-element.196.cos_ref, ...), custom_call_target="tpu_custom_call" | custom-call | tf_op jit(solution)/shard_map/qkv_rotary/pallas_call | solution.py:236
  83.2 35.8 %all_to_all.20 = bf16[8,256,512]{2,1,0:T(8,128)(2,1)} all-to-all(bf16[8,256,512]{2,1,0:T(8,128)(2,1)} %get-tuple-element.79), channel_id=1, replica_groups=mesh['rep'=8,'shard'=16] {'rep'}, dimensions={0} | all-to-all | bytes 4194304 | tf_op jit(solution)/shard_map/all_to_all | solution.py:1167
  119.0 18.0 %attend.1 = (bf16[8,2,128,256]{3,2,1,0:T(8,128)(2,1)}, f32[2,4,512,128]{3,2,1,0:T(8,128)}) custom-call(s32[2]{0:T(128)} %len_ref.3, bf16[8,2,128,512]{3,2,1,0:T(8,128)(2,1)} %bitcast.105), custom_call_target="tpu_custom_call" | custom-call | tf_op jit(solution)/shard_map/attend/pallas_call | solution.py:326
  137.1 3.7 all-to-all-start.1
  141.4 2.2 copy.39
  144.2 13.9 %all-to-all-done.1.o_ref = bf16[8,256,256]{2,1,0:T(8,128)(2,1)S(1)} async-done(((bf16[8,256,256]{2,1,0:T(8,128)(2,1)}), bf16[8,256,256]{2,1,0:T(8,128)(2,1)S(1)}, u32[]{:S(2)}, u32[]{:S(2)}) %all-to-all-start.1) | async-done | bytes 1048608 | tf_op jit(solution)/shard_map/all_to_all | solution.py:1169
  158.1 29.3 %all-gather.7.cloned.1.call-done = bf16[16,704,1024]{2,1,0:T(8,128)(2,1)} async-done(((bf16[2,704,1024]{2,1,0:T(8,128)(2,1)}), bf16[16,704,1024]{2,1,0:T(8,128)(2,1)}) %all-gather.7.cloned.1.call-update) | async-done | bytes 23068688 | tf_op jit(solution)/shard_map/all_gather | solution.py:1019
  187.4 49.4 %token_local.1 = (bf16[256,4096]{1,0:T(8,128)(2,1)}, f32[256,4096]{1,0:T(8,128)}, f32[256,128]{1,0:T(8,128)}, bf16[8,256,256]{2,1,0:T(8,128)(2,1)}, bf16[256,102...) custom-call(s32[3]{0:T(128)} %pad_add_fusion.info_ref, ...), custom_call_target="tpu_custom_call" | custom-call | tf_op jit(solution)/shard_map/token_local/pallas_call | solution.py:707
  236.8 12.7 %weight_grads.1 = bf16[8,2,704,1024]{3,2,1,0:T(8,128)(2,1)} custom-call(bf16[8,256,256]{2,1,0:T(8,128)(2,1)} %copy-done, bf16[256,1024]{1,0:T(8,128)(2,1)} %get-tuple-element.84.dya_ref, bf16[256,1024]{1,0:T(8,128)(2,1)} %get-tuple-element.85.xb_ref, bf16[256,6144]{1,0:T(8,128)(2,1)} %get-tuple-element.86.dgu_ref, ...), custom_call_target="tpu_custom_call" | custom-call | tf_op jit(solution)/shard_map/weight_grads/pallas_call | solution.py:959
  250.8 24.6 %all_to_all.21 = bf16[8,256,256]{2,1,0:T(8,128)(2,1)} all-to-all(bf16[8,256,256]{2,1,0:T(8,128)(2,1)S(1)} %copy-done.9), channel_id=1, replica_groups=mesh['rep'=8,'shard'=16] {'rep'}, dimensions={0} | all-to-all | bytes 2097152 | tf_op jit(solution)/shard_map/all_to_all | solution.py:1186
  275.4 26.6 %attend_back.1 = bf16[8,2,128,512]{3,2,1,0:T(8,128)(2,1)} custom-call(s32[2]{0:T(128)} %len_ref.3, bf16[8,2,128,512]{3,2,1,0:T(8,128)(2,1)} %bitcast.106, bf16[8,2,128,256]{3,2,1,0:T(8,128)(2,1)} %bitcast.113, f32[2,4,512,128]{3,2,1,0:T(8,128)} %get-tuple-element.90.lse_ref), custom_call_target="tpu_custom_call" | custom-call | tf_op jit(solution)/shard_map/attend_back/pallas_call | solution.py:406
  302.0 3.8 all-to-all-start.3
  305.9 28.4 %all-to-all-done.3.d_ref = bf16[8,256,512]{2,1,0:T(8,128)(2,1)S(1)} async-done(((bf16[8,256,512]{2,1,0:T(8,128)(2,1)}), bf16[8,256,512]{2,1,0:T(8,128)(2,1)S(1)}, u32[]{:S(2)}, u32[]{:S(2)}) %all-to-all-start.3) | async-done | bytes 2097184 | tf_op jit(solution)/shard_map/all_to_all | solution.py:1189
  335.7 12.4 %rotary_back.1 = (bf16[8,256,512]{2,1,0:T(8,128)(2,1)}, bf16[8,2,64,4096]{3,2,1,0:T(8,128)(2,1)}, f32[8,128]{1,0:T(8,128)}, f32[8,128]{1,0:T(8,128)}) custom-call(bf16[8,256,512]{2,1,0:T(8,128)(2,1)} %copy-done.1, f32[8,256,384]{2,1,0:T(8,128)} %get-tuple-element.91.u_ref, bf16[256,1024]{1,0:T(8,128)(2,1)} %get-tuple-element.78.x_ref, f32[1,128]{1,0:T(1,128)} %bitcast.148, ...), custom_call_target="tpu_custom_call" | custom-call | tf_op jit(solution)/shard_map/rotary_back/pallas_call | solution.py:792
  348.1 17.1 %lane_in_back.1 = (f32[256,4096]{1,0:T(8,128)}, f32[8,1024]{1,0:T(8,128)}, f32[8,1024]{1,0:T(8,128)}, f32[8,128]{1,0:T(8,128)}) custom-call(bf16[8,256,512]{2,1,0:T(8,128)(2,1)} %get-tuple-element.94.dqkv_ref, bf16[8,2,64,4096]{3,2,1,0:T(8,128)(2,1)} %bitcast.103, bf16[256,4096]{1,0:T(8,128)(2,1)} %bitcast.101, f32[256,128]{1,0:T(8,128)} %get-tuple-element.81.ca_ref.c_ref, ...), custom_call_target="tpu_custom_call" | custom-call | tf_op jit(solution)/shard_map/lane_in_back/pallas_call | solution.py:908
  367.6 4.4 reduce-scatter.3.cloned.1.call-done
  372.1 2.0 select_bitcast_fusion.1
  375.0 1.6 collective-permute-start.16
  376.6 2.2 collective-permute-start.17
  380.2 2.7 collective-permute-done.18
  383.0 9.6 %collective-permute-done.16 = bf16[704,512]{1,0:T(8,128)(2,1)S(1)} collective-permute-done((bf16[704,512]{1,0:T(8,128)(2,1)}, bf16[704,512]{1,0:T(8,128)(2,1)S(1)}, u32[]{:S(2)}, u32[]{:S(2)}) %collective-permute-start.16) | collective-permute-done | bytes 720928 | tf_op jit(solution)/shard_map/ppermute | solution.py:1002
  392.6 2.4 collective-permute-done.17
  395.0 1.7 convert_add_fusion
  397.8 2.8 collective-permute-start.20
  402.3 6.6 %collective-permute-done.21 = f32[116,128]{1,0:T(8,128)S(1)} collective-permute-done((f32[116,128]{1,0:T(8,128)S(1)}, f32[116,128]{1,0:T(8,128)S(1)}, u32[]{:S(2)}, u32[]{:S(2)}) %collective-permute-start.21) | collective-permute-done | bytes 59424 | tf_op jit(solution)/shard_map/ppermute | solution.py:990
  411.5 2.5 collective-permute-start.22
  414.0 2.1 collective-permute-start.24
  416.1 3.7 collective-permute-done.24
  420.8 2.1 collective-permute-start.26
  423.0 1.6 collective-permute-start.25
  425.9 2.0 collective-permute-done.26
  427.9 2.2 collective-permute-done.25
  432.3 3.6 collective-permute-start.30
  435.9 2.2 collective-permute-done.30
  439.4 1.7 collective-permute-start.32
  442.8 1.6 collective-permute-start.33
  444.4 3.0 reshape.496
  447.4 6.0 %reshape.502 = f32[2,128,4,1024]{3,2,1,0:T(4,128)} reshape(f32[256,4096]{1,0:T(8,128)} %get-tuple-element.107) | data formatting | bytes 8388608 | tf_op jit(solution)/shard_map/reshape | solution.py:1228
  465.8 2.1 collective-permute-start.5
  468.4 2.7 collective-permute-done.4
  471.1 2.2 collective-permute-done.5
  473.5 2.7 collective-permute-start.7
  476.2 1.5 collective-permute-start.6
  478.2 1.5 collective-permute-done.7
  481.3 1.5 collective-permute-start.9
  483.7 2.1 collective-permute-done.9
  485.8 2.6 collective-permute-done.8
  488.9 3.2 collective-permute-start.10
  492.2 2.1 collective-permute-done.11
  496.1 3.2 collective-permute-done.13
  503.3 3.7 collective-permute-done.15
  (214 shorter events, 58.0 us)
Async XLA Ops:
  7.2 66.3 %all-gather.5.cloned.1.call-start = ((), (), s32[]{:S(2)}) async-start(), calls=%async_computation.8 | async-start | bytes 9437184 | tf_op jit(solution)/shard_map/all_gather | solution.py:1019
  10.4 8.4 %collective-permute-start = (bf16[64,2048]{1,0:T(8,128)(2,1)S(1)}, bf16[64,2048]{1,0:T(8,128)(2,1)S(1)}, u32[]{:S(2)}, u32[]{:S(2)}) collective-permute-start(bf16[64,2048]{1,0:T(8,128)(2,1)S(1)} %get-tuple-element.171), channel_id=1, source_target_pairs={{0,8},{1,9},{2,10},{3,11},{4,12},{5,13},{6,14},{7,15},{8,0},{9,1},... | collective-permute-start | bytes 786440 | tf_op jit(solution)/shard_map/ppermute | solution.py:1002
  12.5 9.0 %collective-permute-start.1 = (bf16[64,2048]{1,0:T(8,128)(2,1)S(1)}, bf16[64,2048]{1,0:T(8,128)(2,1)S(1)}, u32[]{:S(2)}, u32[]{:S(2)}) collective-permute-start(bf16[64,2048]{1,0:T(8,128)(2,1)S(1)} %get-tuple-element.172), channel_id=1, source_target_pairs={{0,72},{1,73},{2,74},{3,75},{4,76},{5,77},{6,78},{7,79},{8,64},{9,... | collective-permute-start | bytes 786440 | tf_op jit(solution)/shard_map/ppermute | solution.py:1002
  21.7 1.2 copy-start.10
  21.7 1.2 copy-start.6
  22.8 1.0 copy-start.7
  22.8 1.1 copy-start.8
  22.8 164.5 %all-gather.7.cloned.1.call-start = ((), (), s32[]{:S(2)}) async-start(), calls=%async_computation.9 | async-start | bytes 25952256 | tf_op jit(solution)/shard_map/all_gather | solution.py:1019
  24.1 16.8 %collective-permute-start.2 = (bf16[704,512]{1,0:T(8,128)(2,1)S(1)}, bf16[704,512]{1,0:T(8,128)(2,1)S(1)}, u32[]{:S(2)}, u32[]{:S(2)}) collective-permute-start(bf16[704,512]{1,0:T(8,128)(2,1)S(1)} %get-tuple-element.155), channel_id=1, source_target_pairs={{0,8},{1,9},{2,10},{3,11},{4,12},{5,13},{6,14},{7,15},{8,0},{9,1},... | collective-permute-start | bytes 2162696 | tf_op jit(solution)/shard_map/ppermute | solution.py:1002
  24.8 17.9 %collective-permute-start.3 = (bf16[704,512]{1,0:T(8,128)(2,1)S(1)}, bf16[704,512]{1,0:T(8,128)(2,1)S(1)}, u32[]{:S(2)}, u32[]{:S(2)}) collective-permute-start(bf16[704,512]{1,0:T(8,128)(2,1)S(1)} %get-tuple-element.156), channel_id=1, source_target_pairs={{0,72},{1,73},{2,74},{3,75},{4,76},{5,77},{6,78},{7,79},{8,64},{9,... | collective-permute-start | bytes 2162696 | tf_op jit(solution)/shard_map/ppermute | solution.py:1002
  45.2 0.8 copy-start.14
  49.0 3.9 copy-start.20
  49.0 4.6 copy-start.2
  137.1 4.4 copy-start.4
  137.1 21.0 %all-to-all-start.1 = ((bf16[8,256,256]{2,1,0:T(8,128)(2,1)}), bf16[8,256,256]{2,1,0:T(8,128)(2,1)S(1)}, u32[]{:S(2)}, u32[]{:S(2)}) async-start(bf16[8,256,256]{2,1,0:T(8,128)(2,1)} %bitcast.120), calls=%async_computation.1 | async-start | bytes 2097152 | tf_op jit(solution)/shard_map/all_to_all | solution.py:1169
  140.8 231.3 %reduce-scatter.3.cloned.1.call-start = ((), (), s32[]{:S(2)}) async-start(), calls=%async_computation.6 | async-start | bytes 25952256 | tf_op jit(solution)/shard_map/reduce_scatter | solution.py:1023
  141.4 2.2 copy-start.21
  158.1 29.3 %copy-start = (bf16[8,256,256]{2,1,0:T(8,128)(2,1)}, bf16[8,256,256]{2,1,0:T(8,128)(2,1)S(1)}, u32[]{:S(2)}) copy-start(bf16[8,256,256]{2,1,0:T(8,128)(2,1)S(1)} %all-to-all-done.1.o_ref) | copy-start | bytes 3145732
  249.5 1.2 copy-start.9
  302.0 3.8 copy-start.16
  302.0 3.9 copy-start.15
  302.0 3.9 copy-start.17
  302.0 32.3 %all-to-all-start.3 = ((bf16[8,256,512]{2,1,0:T(8,128)(2,1)}), bf16[8,256,512]{2,1,0:T(8,128)(2,1)S(1)}, u32[]{:S(2)}, u32[]{:S(2)}) async-start(bf16[8,256,512]{2,1,0:T(8,128)(2,1)} %bitcast.109), calls=%async_computation.3 | async-start | bytes 4194304 | tf_op jit(solution)/shard_map/all_to_all | solution.py:1189
  305.8 157.5 %reduce-scatter.5.cloned.1.call-start = ((), (), s32[]{:S(2)}) async-start(), calls=%async_computation.7 | async-start | bytes 9437184 | tf_op jit(solution)/shard_map/reduce_scatter | solution.py:1023
  334.3 1.4 copy-start.1
  348.1 17.9 %copy-start.19 = (f32[8,128]{1,0:T(8,128)S(1)}, f32[8,128]{1,0:T(8,128)}, u32[]{:S(2)}) copy-start(f32[8,128]{1,0:T(8,128)} %get-tuple-element.101) | copy-start | bytes 12292
  348.1 17.9 %copy-start.18 = (f32[8,128]{1,0:T(8,128)S(1)}, f32[8,128]{1,0:T(8,128)}, u32[]{:S(2)}) copy-start(f32[8,128]{1,0:T(8,128)} %get-tuple-element.102) | copy-start | bytes 12292
  375.0 17.6 %collective-permute-start.16 = (bf16[704,512]{1,0:T(8,128)(2,1)}, bf16[704,512]{1,0:T(8,128)(2,1)S(1)}, u32[]{:S(2)}, u32[]{:S(2)}) collective-permute-start(bf16[704,512]{1,0:T(8,128)(2,1)} %get-tuple-element.154), channel_id=1, source_target_pairs={{0,8},{1,9},{2,10},{3,11},{4,12},{5,13},{6,14},{7,15},{8,0},{9,1},... | collective-permute-start | bytes 2162696 | tf_op jit(solution)/shard_map/ppermute | solution.py:1002
  376.6 18.4 %collective-permute-start.17 = (bf16[704,512]{1,0:T(8,128)(2,1)S(1)}, bf16[704,512]{1,0:T(8,128)(2,1)}, u32[]{:S(2)}, u32[]{:S(2)}) collective-permute-start(bf16[704,512]{1,0:T(8,128)(2,1)S(1)} %get-tuple-element.153), channel_id=1, source_target_pairs={{0,72},{1,73},{2,74},{3,75},{4,76},{5,77},{6,78},{7,79},{8,64},{9,... | collective-permute-start | bytes 2162696 | tf_op jit(solution)/shard_map/ppermute | solution.py:1002
  378.7 4.2 collective-permute-start.18
  392.6 2.4 copy-start.11
  396.7 1.1 copy-start.3
  397.8 11.0 %collective-permute-start.20 = (bf16[352,512]{1,0:T(8,128)(2,1)S(1)}, bf16[352,512]{1,0:T(8,128)(2,1)S(1)}, u32[]{:S(2)}, u32[]{:S(2)}) collective-permute-start(bf16[352,512]{1,0:T(8,128)(2,1)S(1)} %dynamic-slice_convert_fusion), channel_id=1, source_target_pairs={{0,48},{16,32},{32,16},{48,0},{64,112},{80,96},{96,80},{112,64},{1... | collective-permute-start | bytes 1081352 | tf_op jit(solution)/shard_map/ppermute | solution.py:990
  400.7 8.9 %collective-permute-start.19 = (bf16[352,512]{1,0:T(8,128)(2,1)S(1)}, bf16[352,512]{1,0:T(8,128)(2,1)S(1)}, u32[]{:S(2)}, u32[]{:S(2)}) collective-permute-start(bf16[352,512]{1,0:T(8,128)(2,1)S(1)} %dynamic-slice_convert_fusion.1), channel_id=1, source_target_pairs={{0,16},{16,0},{32,48},{48,32},{64,80},{80,64},{96,112},{112,96},{1... | collective-permute-start | bytes 1081352 | tf_op jit(solution)/shard_map/ppermute | solution.py:990
  401.0 7.9 %collective-permute-start.21 = (f32[116,128]{1,0:T(8,128)S(1)}, f32[116,128]{1,0:T(8,128)S(1)}, u32[]{:S(2)}, u32[]{:S(2)}) collective-permute-start(f32[116,128]{1,0:T(8,128)S(1)} %add.185), channel_id=1, source_target_pairs={{0,48},{16,32},{32,16},{48,0},{64,112},{80,96},{96,80},{112,64},{1... | collective-permute-start | bytes 178184 | tf_op jit(solution)/shard_map/ppermute | solution.py:990
  408.9 0.7 copy-start.12
  411.0 8.8 %collective-permute-start.23 = (bf16[176,512]{1,0:T(8,128)(2,1)S(1)}, bf16[176,512]{1,0:T(8,128)(2,1)}, u32[]{:S(2)}, u32[]{:S(2)}) collective-permute-start(bf16[176,512]{1,0:T(8,128)(2,1)S(1)} %dynamic-slice_convert_fusion.2), channel_id=1, source_target_pairs={{0,16},{16,0},{32,48},{48,32},{64,80},{80,64},{96,112},{112,96},{1... | collective-permute-start | bytes 540680 | tf_op jit(solution)/shard_map/ppermute | solution.py:990
  411.5 8.3 %collective-permute-start.22 = (bf16[176,512]{1,0:T(8,128)(2,1)S(1)}, bf16[176,512]{1,0:T(8,128)(2,1)S(1)}, u32[]{:S(2)}, u32[]{:S(2)}) collective-permute-start(bf16[176,512]{1,0:T(8,128)(2,1)S(1)} %dynamic-slice_convert_fusion.3), channel_id=1, source_target_pairs={{0,48},{16,32},{32,16},{48,0},{64,112},{80,96},{96,80},{112,64},{1... | collective-permute-start | bytes 540680 | tf_op jit(solution)/shard_map/ppermute | solution.py:990
  414.0 5.8 %collective-permute-start.24 = (f32[116,128]{1,0:T(8,128)S(1)}, f32[116,128]{1,0:T(8,128)S(1)}, u32[]{:S(2)}, u32[]{:S(2)}) collective-permute-start(f32[116,128]{1,0:T(8,128)S(1)} %add.192), channel_id=1, source_target_pairs={{0,64},{16,80},{32,96},{48,112},{64,0},{80,16},{96,32},{112,48},{1... | collective-permute-start | bytes 178184 | tf_op jit(solution)/shard_map/ppermute | solution.py:1029
  420.8 7.1 %collective-permute-start.26 = (bf16[176,512]{1,0:T(8,128)(2,1)S(1)}, bf16[176,512]{1,0:T(8,128)(2,1)S(1)}, u32[]{:S(2)}, u32[]{:S(2)}) collective-permute-start(bf16[176,512]{1,0:T(8,128)(2,1)S(1)} %add_convert_fusion.2), channel_id=1, source_target_pairs={{0,64},{16,80},{32,96},{48,112},{64,0},{80,16},{96,32},{112,48},{1... | collective-permute-start | bytes 540680 | tf_op jit(solution)/shard_map/ppermute | solution.py:1029
  423.0 7.1 %collective-permute-start.25 = (bf16[176,512]{1,0:T(8,128)(2,1)S(1)}, bf16[176,512]{1,0:T(8,128)(2,1)S(1)}, u32[]{:S(2)}, u32[]{:S(2)}) collective-permute-start(bf16[176,512]{1,0:T(8,128)(2,1)S(1)} %add_convert_fusion.3), channel_id=1, source_target_pairs={{0,64},{16,80},{32,96},{48,112},{64,0},{80,16},{96,32},{112,48},{1... | collective-permute-start | bytes 540680 | tf_op jit(solution)/shard_map/ppermute | solution.py:1029
  424.5 1.3 collective-permute-start.27
  430.1 8.0 %collective-permute-start.29 = (bf16[176,512]{1,0:T(8,128)(2,1)S(1)}, bf16[176,512]{1,0:T(8,128)(2,1)S(1)}, u32[]{:S(2)}, u32[]{:S(2)}) collective-permute-start(bf16[176,512]{1,0:T(8,128)(2,1)S(1)} %add_convert_fusion), channel_id=1, source_target_pairs={{0,16},{16,0},{32,48},{48,32},{64,80},{80,64},{96,112},{112,96},{1... | collective-permute-start | bytes 540680 | tf_op jit(solution)/shard_map/ppermute | solution.py:990
  431.6 7.1 %collective-permute-start.28 = (bf16[176,512]{1,0:T(8,128)(2,1)S(1)}, bf16[176,512]{1,0:T(8,128)(2,1)S(1)}, u32[]{:S(2)}, u32[]{:S(2)}) collective-permute-start(bf16[176,512]{1,0:T(8,128)(2,1)S(1)} %add_convert_fusion.1), channel_id=1, source_target_pairs={{0,48},{16,32},{32,16},{48,0},{64,112},{80,96},{96,80},{112,64},{1... | collective-permute-start | bytes 540680 | tf_op jit(solution)/shard_map/ppermute | solution.py:990
  432.3 5.8 %collective-permute-start.30 = (f32[116,128]{1,0:T(8,128)S(1)}, f32[116,128]{1,0:T(8,128)S(1)}, u32[]{:S(2)}, u32[]{:S(2)}) collective-permute-start(f32[116,128]{1,0:T(8,128)S(1)} %add.199), channel_id=1, source_target_pairs={{0,2},{1,3},{2,0},{3,1},{4,6},{5,7},{6,4},{7,5},{8,10},{9,11},{10,... | collective-permute-start | bytes 178184 | tf_op jit(solution)/shard_map/ppermute | solution.py:1070
  435.9 8.4 %copy-start.5 = (bf16[256,4096]{1,0:T(8,128)(2,1)S(1)}, bf16[256,4096]{1,0:T(8,128)(2,1)}, u32[]{:S(2)}) copy-start(bf16[256,4096]{1,0:T(8,128)(2,1)} %get-tuple-element.82) | copy-start | bytes 6291460
  438.8 0.7 copy-start.13
  439.4 13.9 %collective-permute-start.32 = (bf16[352,512]{1,0:T(8,128)(2,1)S(1)}, bf16[352,512]{1,0:T(8,128)(2,1)}, u32[]{:S(2)}, u32[]{:S(2)}) collective-permute-start(bf16[352,512]{1,0:T(8,128)(2,1)S(1)} %pad_maximum_fusion.5), channel_id=1, source_target_pairs={{0,48},{16,32},{32,16},{48,0},{64,112},{80,96},{96,80},{112,64},{1... | collective-permute-start | bytes 1081352 | tf_op jit(solution)/shard_map/ppermute | solution.py:990
  442.8 10.6 %collective-permute-start.31 = (bf16[352,512]{1,0:T(8,128)(2,1)}, bf16[352,512]{1,0:T(8,128)(2,1)}, u32[]{:S(2)}, u32[]{:S(2)}) collective-permute-start(bf16[352,512]{1,0:T(8,128)(2,1)} %pad_maximum_fusion.4), channel_id=1, source_target_pairs={{0,16},{16,0},{32,48},{48,32},{64,80},{80,64},{96,112},{112,96},{1... | collective-permute-start | bytes 1081352 | tf_op jit(solution)/shard_map/ppermute | solution.py:990
  442.8 10.6 %collective-permute-start.33 = (f32[116,128]{1,0:T(8,128)S(1)}, f32[116,128]{1,0:T(8,128)S(1)}, u32[]{:S(2)}, u32[]{:S(2)}) collective-permute-start(f32[116,128]{1,0:T(8,128)S(1)} %add.200), channel_id=1, source_target_pairs={{0,6},{1,7},{2,4},{3,5},{4,2},{5,3},{6,0},{7,1},{8,14},{9,15},{10,... | collective-permute-start | bytes 178184 | tf_op jit(solution)/shard_map/ppermute | solution.py:1070
  453.4 9.9 %collective-permute-start.34 = (f32[116,128]{1,0:T(8,128)S(1)}, f32[116,128]{1,0:T(8,128)S(1)}, u32[]{:S(2)}, u32[]{:S(2)}) collective-permute-start(f32[116,128]{1,0:T(8,128)S(1)} %add.201), channel_id=1, source_target_pairs={{0,8},{1,9},{2,10},{3,11},{4,12},{5,13},{6,14},{7,15},{8,0},{9,1},... | collective-permute-start | bytes 178184 | tf_op jit(solution)/shard_map/ppermute | solution.py:1029
  464.7 6.5 %collective-permute-start.4 = (bf16[64,2048]{1,0:T(8,128)(2,1)S(1)}, bf16[64,2048]{1,0:T(8,128)(2,1)S(1)}, u32[]{:S(2)}, u32[]{:S(2)}) collective-permute-start(bf16[64,2048]{1,0:T(8,128)(2,1)S(1)} %get-tuple-element.170), channel_id=1, source_target_pairs={{0,8},{1,9},{2,10},{3,11},{4,12},{5,13},{6,14},{7,15},{8,0},{9,1},... | collective-permute-start | bytes 786440 | tf_op jit(solution)/shard_map/ppermute | solution.py:1002
  465.8 7.6 %collective-permute-start.5 = (bf16[64,2048]{1,0:T(8,128)(2,1)S(1)}, bf16[64,2048]{1,0:T(8,128)(2,1)S(1)}, u32[]{:S(2)}, u32[]{:S(2)}) collective-permute-start(bf16[64,2048]{1,0:T(8,128)(2,1)S(1)} %get-tuple-element.169), channel_id=1, source_target_pairs={{0,72},{1,73},{2,74},{3,75},{4,76},{5,77},{6,78},{7,79},{8,64},{9,... | collective-permute-start | bytes 786440 | tf_op jit(solution)/shard_map/ppermute | solution.py:1002
  473.5 6.3 %collective-permute-start.7 = (bf16[32,2048]{1,0:T(8,128)(2,1)S(1)}, bf16[32,2048]{1,0:T(8,128)(2,1)S(1)}, u32[]{:S(2)}, u32[]{:S(2)}) collective-permute-start(bf16[32,2048]{1,0:T(8,128)(2,1)S(1)} %dynamic-slice_convert_fusion.4), channel_id=1, source_target_pairs={{0,48},{16,32},{32,16},{48,0},{64,112},{80,96},{96,80},{112,64},{1... | collective-permute-start | bytes 393224 | tf_op jit(solution)/shard_map/ppermute | solution.py:990
  476.2 5.0 collective-permute-start.6
  481.3 4.5 collective-permute-start.9
  482.9 5.6 %collective-permute-start.8 = (bf16[16,2048]{1,0:T(8,128)(2,1)S(1)}, bf16[16,2048]{1,0:T(8,128)(2,1)S(1)}, u32[]{:S(2)}, u32[]{:S(2)}) collective-permute-start(bf16[16,2048]{1,0:T(8,128)(2,1)S(1)} %dynamic-slice_convert_fusion.7), channel_id=1, source_target_pairs={{0,48},{16,32},{32,16},{48,0},{64,112},{80,96},{96,80},{112,64},{1... | collective-permute-start | bytes 196616 | tf_op jit(solution)/shard_map/ppermute | solution.py:990
  488.4 5.8 %collective-permute-start.11 = (bf16[16,2048]{1,0:T(8,128)(2,1)S(1)}, bf16[16,2048]{1,0:T(8,128)(2,1)S(1)}, u32[]{:S(2)}, u32[]{:S(2)}) collective-permute-start(bf16[16,2048]{1,0:T(8,128)(2,1)S(1)} %add_convert_fusion.6), channel_id=1, source_target_pairs={{0,64},{16,80},{32,96},{48,112},{64,0},{80,16},{96,32},{112,48},{1... | collective-permute-start | bytes 196616 | tf_op jit(solution)/shard_map/ppermute | solution.py:1029
  488.9 6.0 %collective-permute-start.10 = (bf16[16,2048]{1,0:T(8,128)(2,1)S(1)}, bf16[16,2048]{1,0:T(8,128)(2,1)S(1)}, u32[]{:S(2)}, u32[]{:S(2)}) collective-permute-start(bf16[16,2048]{1,0:T(8,128)(2,1)S(1)} %add_convert_fusion.7), channel_id=1, source_target_pairs={{0,64},{16,80},{32,96},{48,112},{64,0},{80,16},{96,32},{112,48},{1... | collective-permute-start | bytes 196616 | tf_op jit(solution)/shard_map/ppermute | solution.py:1029
  495.0 4.3 collective-permute-start.13
  495.1 5.6 %collective-permute-start.12 = (bf16[16,2048]{1,0:T(8,128)(2,1)S(1)}, bf16[16,2048]{1,0:T(8,128)(2,1)S(1)}, u32[]{:S(2)}, u32[]{:S(2)}) collective-permute-start(bf16[16,2048]{1,0:T(8,128)(2,1)S(1)} %add_convert_fusion.5), channel_id=1, source_target_pairs={{0,48},{16,32},{32,16},{48,0},{64,112},{80,96},{96,80},{112,64},{1... | collective-permute-start | bytes 196616 | tf_op jit(solution)/shard_map/ppermute | solution.py:990
  500.7 6.3 %collective-permute-start.15 = (bf16[32,2048]{1,0:T(8,128)(2,1)S(1)}, bf16[32,2048]{1,0:T(8,128)(2,1)S(1)}, u32[]{:S(2)}, u32[]{:S(2)}) collective-permute-start(bf16[32,2048]{1,0:T(8,128)(2,1)S(1)} %pad_maximum_fusion.9), channel_id=1, source_target_pairs={{0,48},{16,32},{32,16},{48,0},{64,112},{80,96},{96,80},{112,64},{1... | collective-permute-start | bytes 393224 | tf_op jit(solution)/shard_map/ppermute | solution.py:990
  501.8 5.2 %collective-permute-start.14 = (bf16[32,2048]{1,0:T(8,128)(2,1)S(1)}, bf16[32,2048]{1,0:T(8,128)(2,1)S(1)}, u32[]{:S(2)}, u32[]{:S(2)}) collective-permute-start(bf16[32,2048]{1,0:T(8,128)(2,1)S(1)} %pad_maximum_fusion.8), channel_id=1, source_target_pairs={{0,16},{16,0},{32,48},{48,32},{64,80},{80,64},{96,112},{112,96},{1... | collective-permute-start | bytes 393224 | tf_op jit(solution)/shard_map/ppermute | solution.py:990
Sparse Core Ops, SparseCore 0:
  22.9 50.5 all-gather.4
  75.8 111.5 all-gather.6
  249.7 122.3 reduce-scatter.2
  374.3 51.9 reduce-scatter.4

commit v2 on v1

--- a/solution.py
+++ b/solution.py
@@ -519,7 +519,7 @@
     def chunk(step):
         return pl.ds(pl.multiple_of(step * CHUNK, CHUNK), CHUNK)
 
-    tile = 256
+    tile = 512
 
     def tile_at(n):
         return pl.ds(pl.multiple_of(n * tile, tile), tile)
@@ -835,7 +835,7 @@
 ):
     groups, rows, span = dqkv_ref.shape
     width = gain_ref.shape[1]
-    tile = 256
+    tile = 512
 
     per = tile // w_ref.shape[2]
     half_tiles = width // tile // 2
@@ -974,6 +974,89 @@
     )(o, dya, xb, dgu, hid, dyb)
 
 
+def group_kernel(q_ref, k_ref, v_ref, out_ref, *, hd):
+    groups = k_ref.shape[1] // hd
+    for g in range(groups):
+        at = 4 * hd * g
+        out_ref[:, at : at + 2 * hd] = q_ref[:, 2 * hd * g : 2 * hd * (g + 1)]
+        out_ref[:, at + 2 * hd : at + 3 * hd] = k_ref[:, hd * g : hd * (g + 1)]
+        out_ref[:, at + 3 * hd : at + 4 * hd] = v_ref[:, hd * g : hd * (g + 1)]
+
+
+def group_columns(q, k, v, hd):
+    vm = pl.BlockSpec(memory_space=pltpu.VMEM)
+    columns = q.shape[1] + k.shape[1] + v.shape[1]
+    return pl.pallas_call(
+        partial(group_kernel, hd=hd),
+        in_specs=[vm] * 3,
+        out_specs=vm,
+        out_shape=jax.ShapeDtypeStruct((q.shape[0], columns), BF16),
+        compiler_params=params(),
+        name="group_columns",
+    )(q, k, v)
+
+
+def ungroup_kernel(place_ref, *refs, hd):
+    pieces, (q_ref, k_ref, v_ref) = refs[:RING], refs[RING:]
+    groups = k_ref.shape[1] // hd
+    rows = pieces[0].shape[0]
+    for d, x_ref in enumerate(pieces):
+        at = pl.multiple_of(lax.rem(place_ref[0] + RING - d, RING) * rows, rows)
+        rs = pl.ds(at, rows)
+        for g in range(groups):
+            cs = 4 * hd * g
+            q_ref[rs, 2 * hd * g : 2 * hd * (g + 1)] = x_ref[:, cs : cs + 2 * hd].astype(F32)
+            k_ref[rs, hd * g : hd * (g + 1)] = x_ref[:, cs + 2 * hd : cs + 3 * hd].astype(F32)
+            v_ref[rs, hd * g : hd * (g + 1)] = x_ref[:, cs + 3 * hd : cs + 4 * hd].astype(F32)
+
+
+def ungroup_columns(place, pieces, hd):
+    vm = pl.BlockSpec(memory_space=pltpu.VMEM)
+    rows, columns = pieces[0].shape
+    return pl.pallas_call(
+        partial(ungroup_kernel, hd=hd),
+        in_specs=[pl.BlockSpec(memory_space=pltpu.SMEM)] + [vm] * RING,
+        out_specs=[vm] * 3,
+        out_shape=[
+            jax.ShapeDtypeStruct((RING * rows, columns // part), F32) for part in (2, 4, 4)
+        ],
+        compiler_params=params(),
+        name="ungroup_columns",
+    )(place, *pieces)
+
+
+def split_kernel(x_ref, out_ref, gate_ref, up_ref, down_ref):
+    width = x_ref.shape[1]
+    at = out_ref.shape[0]
+    out_ref[...] = x_ref[0:at].astype(F32)
+    for ref in (gate_ref, up_ref):
+        local, ff = ref.shape
+        for t in range(ff // width):
+            ref[:, t * width : (t + 1) * width] = x_ref[at : at + local].astype(F32)
+            at += local
+    down_ref[...] = x_ref[at:].astype(F32)
+
+
+def split_rows(x, out_rows, local, ff):
+    vm = pl.BlockSpec(memory_space=pltpu.VMEM)
+    rows, width = x.shape
+    down = rows - out_rows - 2 * local * (ff // width)
+    sds = jax.ShapeDtypeStruct
+    return pl.pallas_call(
+        split_kernel,
+        in_specs=[vm],
+        out_specs=[vm] * 4,
+        out_shape=[
+            sds((out_rows, width), F32),
+            sds((local, ff), F32),
+            sds((local, ff), F32),
+            sds((down, width), F32),
+        ],
+        compiler_params=params(),
+        name="split_rows",
+    )(x)
+
+
 RING = 4
 
 
@@ -988,6 +1071,11 @@
 
 def swap_y(values, kind):
     return lax.ppermute(values, "rep", pair_along(kind, lax.axis_size("rep"), 1))
+
+
+def shift_y(values, step):
+    pairs = [(r, r // RING * RING + (r + step) % RING) for r in range(lax.axis_size("rep"))]
+    return lax.ppermute(values, "rep", pairs)
 
 
 def swap_z(values, kind):
@@ -1063,6 +1151,34 @@
     return jnp.concatenate(low, axis=1)
 
 
+def rep_sum_short(pair):
+    first = z_place() == 0
+    values = jnp.where(first, pair[0], pair[1])
+    others = jnp.where(first, pair[1], pair[0])
+    place = lax.axis_index("rep") % RING
+    mid = values.shape[1] // 2
+    got = yield [
+        (partial(swap_z, kind=0), others[:, :mid]),
+        (partial(swap_z, kind=1), others[:, mid:]),
+    ]
+    acc = values.astype(F32) + jnp.concatenate(got, axis=1).astype(F32)
+    rows = acc.shape[0] // RING
+
+    def quarter(d):
+        return lax.dynamic_slice_in_dim(acc, (place + d) % RING * rows, rows, 0)
+
+    shifts = range(1, RING)
+    got = yield [(partial(shift_y, step=d), quarter(d).astype(BF16)) for d in shifts]
+    acc = quarter(0)
+    for g in got:
+        acc = acc + g.astype(F32)
+    low = acc.astype(BF16)
+    (got,) = yield [(partial(swap_xor, axis="rep", stride=RING), low)]
+    low = (low.astype(F32) + got.astype(F32)).astype(BF16)
+    got = yield [(partial(shift_y, step=d), low) for d in shifts]
+    return [low] + list(got)
+
+
 def sum_everywhere(values):
     pairs = partial(pair_along, count=lax.axis_size("shard"), stride=2)
     swaps = [partial(swap_y, kind=0), partial(swap_y, kind=1)]
@@ -1077,14 +1193,18 @@
 
 def rounds(*chains):
     results = [None] * len(chains)
-    asked = {n: next(chain) for n, chain in enumerate(chains)}
-    while asked:
+    asked, waiting, at = {}, dict(enumerate(chains)), 0
+    while asked or waiting:
+        for n, (ahead, chain) in list(waiting.items()):
+            if ahead <= at:
+                asked[n] = next(chain)
+                del waiting[n]
         got = {n: [swap(value) for swap, value in wants] for n, wants in asked.items()}
         got = lax.optimization_barrier(got)
-        asked = {}
+        asked, at = {}, at + 1
         for n, values in got.items():
             try:
-                asked[n] = chains[n].send(values)
+                asked[n] = chains[n][1].send(values)
             except StopIteration as end:
                 results[n] = end.value
     return results
@@ -1134,14 +1254,7 @@
     tiles = ff // width
     first = lax.axis_index("rep") * places
 
-    grouped = jnp.concatenate(
-        [
-            w_query.reshape(local, groups, 2 * hd),
-            w_key.reshape(local, groups, hd),
-            w_value.reshape(local, groups, hd),
-        ],
-        axis=2,
-    ).reshape(local, groups * 4 * hd)
+    grouped = group_columns(w_query, w_key, w_value, hd)
     w_grouped = gather_rows(grouped)
     rest = jnp.concatenate(
         [w_out]
@@ -1204,16 +1317,18 @@
             dstatic_b.sum(0),
         ]
     ).reshape(-1, PACK)
-    qkv_part, rest_own, dres, small = lax.optimization_barrier((qkv_part, rest_own, dres, small))
+    dres, out = dres.reshape(residuals.shape), out.reshape(residuals.shape)
+    qkv_part, rest_own, dres, out, small = lax.optimization_barrier(
+        (qkv_part, rest_own, dres, out, small)
+    )
     qkv_own = scatter_rows(qkv_part)
-    rest_low, small = rounds(rep_sum(rest_own), sum_everywhere(small))
-    rest_sum = rest_low.astype(F32)
-    at, edge = w_out.shape[0], w_out.shape[0] + 2 * tiles * local
-    gu = rest_sum[at:edge].reshape(2, tiles, local, width).transpose(0, 2, 1, 3)
-    gu = gu.reshape(2, local, ff)
+    rest_low, small, qkv_low = rounds(
+        (0, rep_sum(rest_own)), (0, sum_everywhere(small)), (3, rep_sum_short(qkv_own))
+    )
+    grad_out, grad_gate, grad_up, grad_down = split_rows(rest_low, w_out.shape[0], local, ff)
+    place = (lax.axis_index("rep") % RING).astype(jnp.int32)[None]
+    grad_query, grad_key, grad_value = ungroup_columns(place, qkv_low, hd)
     small = small.reshape(-1)
-    (qkv_low,) = rounds(rep_sum(qkv_own))
-    qkv_sum = qkv_low.astype(F32).reshape(local, groups, 4 * hd)
     sizes = [width, width, hd, hd, count * width, count * width, PACK, PACK]
     pieces, start = [], 0
     for size in sizes:
@@ -1224,15 +1339,15 @@
         return flat[: 8 * lane_count].reshape(lane_count, 8)[:, :count]
 
     return (
-        out.reshape(residuals.shape),
-        dres.reshape(residuals.shape),
-        qkv_sum[:, :, : 2 * hd].reshape(local, -1),
-        qkv_sum[:, :, 2 * hd : 3 * hd].reshape(local, -1),
-        qkv_sum[:, :, 3 * hd :].reshape(local, -1),
-        rest_sum[:at],
-        gu[0],
-        gu[1],
-        rest_sum[edge:],
+        out,
+        dres,
+        grad_query,
+        grad_key,
+        grad_value,
+        grad_out,
+        grad_gate,
+        grad_up,
+        grad_down,
         pieces[0],
         pieces[1],
         pieces[2],

time: 526 us -> 495 us (0.941)
  waiting for transfers between devices: 167 us -> 153 us
  local copies, waits for them, and re-layouts: 39.7 us -> 32.7 us
  starting transfers between devices: 59.2 us -> 52.9 us
  other arithmetic: 22.8 us -> 16.7 us
    ppermute x18 -> x10, waiting for transfers between devices: 26 us -> 12.7 us  [swap_y(): lax.ppermute(values, 'rep', pair_along(kind, lax.axis_size('rep'), 1))]
    ppermute x18 -> x10, starting transfers between devices: 21.3 us -> 13.1 us  [swap_y(): lax.ppermute(values, 'rep', pair_along(kind, lax.axis_size('rep'), 1))]
    unnamed x79 -> x87, local copies, waits for them, and re-layouts: 21.9 us -> 14.6 us
    pallas_call x0 -> x3, Pallas kernels: none -> 7 us  [the longest x1 2.98 us: split_rows(): pl.pallas_call(split_kernel, in_specs=[vm], out_specs=[vm] * 4, out_shape...]
    ppermute x0 -> x6, starting transfers between devices: none -> 6.77 us  [shift_y(): return lax.ppermute(values, 'rep', pairs)]
    ppermute x0 -> x6, waiting for transfers between devices: none -> 6.31 us  [shift_y(): return lax.ppermute(values, 'rep', pairs)]
    ppermute x7 -> x6, starting transfers between devices: 10.7 us -> 8.35 us  [swap_xor(): lax.ppermute(values, axis, [(i, i ^ stride) for i in range(lax.axis_size(...]
    ppermute x7 -> x6, waiting for transfers between devices: 11.9 us -> 12.6 us  [swap_xor(): lax.ppermute(values, axis, [(i, i ^ stride) for i in range(lax.axis_size(...]
  transfers between devices with their start and end apart: 41 -> 38, of which waited for: 30 -> 20; matrix products, arithmetic and copies ran while one was open for 9% -> 8% of each run, Pallas kernels for 18% -> 19%
where the time goes in v2:
time: 495 us; the launch traced here: 488 us
  Pallas kernels  158 us (32%)
  waiting for transfers between devices  153 us (31%)
  blocking collectives  60.2 us (12%)
  starting transfers between devices  52.9 us (11%)
  local copies, waits for them, and re-layouts  32.7 us (7%)
  other arithmetic  16.7 us (3%)
  between operations  15 us (3%)
    pallas_call x1, Pallas kernels, middle(): pl.pallas_call(middle_kernel, in_specs=[pl.BlockSpec(memory_space=pltpu.S...  46.9 us
    all_gather x2, waiting for transfers between devices, gather_rows(): return lax.all_gather(pair, 'shard', axis_index_groups=z_groups())  41.4 us
    all_to_all x1, blocking collectives, on_device(): lax.all_to_all(send, 'rep', 0, 0, tiled=True)  35.8 us
    ppermute x8, waiting for transfers between devices, swap_z(): return lax.ppermute(values, ('rep', 'shard'), pairs)  34.4 us
    pallas_call x1, Pallas kernels, attend_back(): pl.pallas_call(attend_back_kernel, grid=(pairs,), in_specs=[pl.BlockSpec(...  26.7 us
    all_to_all x1, blocking collectives, on_device(): lax.all_to_all(do, 'rep', 0, 0, tiled=True)  24.4 us
    all_to_all x1, waiting for transfers between devices, on_device(): lax.all_to_all(d_own.reshape(rep, rows, 4 * hd), 'rep', 0, 0, tiled=True)  23.8 us
    pallas_call x1, Pallas kernels, attend(): pl.pallas_call(attend_kernel, grid=(pairs,), in_specs=[pl.BlockSpec(memor...  18 us
  transfers between devices with their start and end apart: 38, of which 20 were waited for; matrix products, arithmetic and copies ran while one was open for 8% of the time, Pallas kernels for 19%

profile of v2, /device:TPU:0, one launch (start us, length us, event | category | flops | bytes accessed | tf_op | source)
XLA Modules:
  0.0 487.8 jit_solution(6230842389633233238)
XLA Ops:
  7.2 1.9 group_columns.1
  10.3 2.1 collective-permute-start
  12.3 2.5 collective-permute-start.1
  14.9 3.8 collective-permute-done
  18.7 2.6 collective-permute-done.1
  24.5 2.3 collective-permute-start.3
  27.0 13.6 %collective-permute-done.2 = bf16[704,512]{1,0:T(8,128)(2,1)S(1)} collective-permute-done((bf16[704,512]{1,0:T(8,128)(2,1)S(1)}, bf16[704,512]{1,0:T(8,128)(2,1)S(1)}, u32[]{:S(2)}, u32[]{:S(2)}) %collective-permute-start.2) | collective-permute-done | bytes 720928 | tf_op jit(solution)/shard_map/ppermute | solution.py:1090
  40.6 1.8 collective-permute-done.3
  43.1 1.8 pad_maximum_fusion
  46.4 2.3 pack_hyper_weights.1
  48.7 3.9 copy.33
  53.3 1.6 slice_bitcast_fusion
  54.9 5.2 %lane_in_zero.1 = (bf16[256,1024]{1,0:T(8,128)(2,1)}, f32[256,128]{1,0:T(8,128)}, f32[256,128]{1,0:T(8,128)}) custom-call(bf16[256,4096]{1,0:T(8,128)(2,1)} %bitcast.75, bf16[4,128,1024]{2,1,0:T(8,128)(2,1)} %get-tuple-element.160.w_ref.wrow_ref, f32[1,128]{1,0:T(1,128)} %pad.15.static_ref, f32[1,1024]{1,0:T(1,128)} %bitcast.98), custom_call_target="tpu_custom_call" | custom-call | tf_op jit(solution)/shard_map/lane_in_zero/pallas_call | solution.py:180
  61.2 12.1 %all-gather.5.cloned.1.call-done = bf16[16,64,4096]{2,1,0:T(8,128)(2,1)} async-done(((bf16[2,64,4096]{2,1,0:T(8,128)(2,1)}), bf16[16,64,4096]{2,1,0:T(8,128)(2,1)}) %all-gather.5.cloned.1.call-update) | async-done | bytes 8388624 | tf_op jit(solution)/shard_map/all_gather | solution.py:1107
  73.3 9.7 %qkv_rotary.1 = (bf16[8,256,512]{2,1,0:T(8,128)(2,1)}, f32[8,256,384]{2,1,0:T(8,128)}) custom-call(bf16[256,1024]{1,0:T(8,128)(2,1)} %get-tuple-element.84.x_ref, bf16[8,2,64,4096]{3,2,1,0:T(8,128)(2,1)} %bitcast.78, f32[1,128]{1,0:T(1,128)} %bitcast.101, f32[1,128]{1,0:T(1,128)} %bitcast.103, f32[128,128]{1,0:T(8,128)} %get-tuple-element.195.cos_ref, ...), custom_call_target="tpu_custom_call" | custom-call | tf_op jit(solution)/shard_map/qkv_rotary/pallas_call | solution.py:236
  82.9 35.8 %all_to_all.20 = bf16[8,256,512]{2,1,0:T(8,128)(2,1)} all-to-all(bf16[8,256,512]{2,1,0:T(8,128)(2,1)} %get-tuple-element.85), channel_id=1, replica_groups=mesh['rep'=8,'shard'=16] {'rep'}, dimensions={0} | all-to-all | bytes 4194304 | tf_op jit(solution)/shard_map/all_to_all | solution.py:1280
  118.8 18.0 %attend.1 = (bf16[8,2,128,256]{3,2,1,0:T(8,128)(2,1)}, f32[2,4,512,128]{3,2,1,0:T(8,128)}) custom-call(s32[2]{0:T(128)} %len_ref.3, bf16[8,2,128,512]{3,2,1,0:T(8,128)(2,1)} %bitcast.81), custom_call_target="tpu_custom_call" | custom-call | tf_op jit(solution)/shard_map/attend/pallas_call | solution.py:326
  136.8 3.7 all-to-all-start.1
  141.2 2.2 copy.34
  143.9 13.9 %all-to-all-done.1.o_ref = bf16[8,256,256]{2,1,0:T(8,128)(2,1)S(1)} async-done(((bf16[8,256,256]{2,1,0:T(8,128)(2,1)}), bf16[8,256,256]{2,1,0:T(8,128)(2,1)S(1)}, u32[]{:S(2)}, u32[]{:S(2)}) %all-to-all-start.1) | async-done | bytes 1048608 | tf_op jit(solution)/shard_map/all_to_all | solution.py:1282
  157.8 29.3 %all-gather.7.cloned.1.call-done = bf16[16,704,1024]{2,1,0:T(8,128)(2,1)} async-done(((bf16[2,704,1024]{2,1,0:T(8,128)(2,1)}), bf16[16,704,1024]{2,1,0:T(8,128)(2,1)}) %all-gather.7.cloned.1.call-update) | async-done | bytes 23068688 | tf_op jit(solution)/shard_map/all_gather | solution.py:1107
  187.1 46.9 %token_local.1 = (bf16[256,4096]{1,0:T(8,128)(2,1)}, f32[256,4096]{1,0:T(8,128)}, f32[256,128]{1,0:T(8,128)}, bf16[8,256,256]{2,1,0:T(8,128)(2,1)}, bf16[256,102...) custom-call(s32[3]{0:T(128)} %pad_add_fusion.info_ref, ...), custom_call_target="tpu_custom_call" | custom-call | tf_op jit(solution)/shard_map/token_local/pallas_call | solution.py:707
  234.0 13.0 %weight_grads.1 = bf16[8,2,704,1024]{3,2,1,0:T(8,128)(2,1)} custom-call(bf16[8,256,256]{2,1,0:T(8,128)(2,1)} %copy-done, bf16[256,1024]{1,0:T(8,128)(2,1)} %get-tuple-element.89.dya_ref, bf16[256,1024]{1,0:T(8,128)(2,1)} %get-tuple-element.90.xb_ref, bf16[256,6144]{1,0:T(8,128)(2,1)} %get-tuple-element.91.dgu_ref, ...), custom_call_target="tpu_custom_call" | custom-call | tf_op jit(solution)/shard_map/weight_grads/pallas_call | solution.py:959
  248.2 24.4 %all_to_all.21 = bf16[8,256,256]{2,1,0:T(8,128)(2,1)} all-to-all(bf16[8,256,256]{2,1,0:T(8,128)(2,1)S(1)} %copy-done.12), channel_id=1, replica_groups=mesh['rep'=8,'shard'=16] {'rep'}, dimensions={0} | all-to-all | bytes 2097152 | tf_op jit(solution)/shard_map/all_to_all | solution.py:1299
  272.6 26.7 %attend_back.1 = bf16[8,2,128,512]{3,2,1,0:T(8,128)(2,1)} custom-call(s32[2]{0:T(128)} %len_ref.3, bf16[8,2,128,512]{3,2,1,0:T(8,128)(2,1)} %bitcast.82, bf16[8,2,128,256]{3,2,1,0:T(8,128)(2,1)} %bitcast.85, f32[2,4,512,128]{3,2,1,0:T(8,128)} %get-tuple-element.95.lse_ref), custom_call_target="tpu_custom_call" | custom-call | tf_op jit(solution)/shard_map/attend_back/pallas_call | solution.py:406
  299.2 3.8 all-to-all-start.3
  303.1 4.5 reshape.390
  307.7 23.8 %all-to-all-done.3.d_ref = bf16[8,256,512]{2,1,0:T(8,128)(2,1)S(1)} async-done(((bf16[8,256,512]{2,1,0:T(8,128)(2,1)}), bf16[8,256,512]{2,1,0:T(8,128)(2,1)S(1)}, u32[]{:S(2)}, u32[]{:S(2)}) %all-to-all-start.3) | async-done | bytes 2097184 | tf_op jit(solution)/shard_map/all_to_all | solution.py:1302
  331.5 1.4 copy-done.1
  332.8 12.4 %rotary_back.1 = (bf16[8,256,512]{2,1,0:T(8,128)(2,1)}, bf16[8,2,64,4096]{3,2,1,0:T(8,128)(2,1)}, f32[8,128]{1,0:T(8,128)}, f32[8,128]{1,0:T(8,128)}) custom-call(bf16[8,256,512]{2,1,0:T(8,128)(2,1)} %copy-done.1, f32[8,256,384]{2,1,0:T(8,128)} %get-tuple-element.96.u_ref, bf16[256,1024]{1,0:T(8,128)(2,1)} %get-tuple-element.84.x_ref, f32[1,128]{1,0:T(1,128)} %bitcast.102, ...), custom_call_target="tpu_custom_call" | custom-call | tf_op jit(solution)/shard_map/rotary_back/pallas_call | solution.py:792
  345.3 16.6 %lane_in_back.1 = (f32[256,4096]{1,0:T(8,128)}, f32[8,1024]{1,0:T(8,128)}, f32[8,1024]{1,0:T(8,128)}, f32[8,128]{1,0:T(8,128)}) custom-call(bf16[8,256,512]{2,1,0:T(8,128)(2,1)} %get-tuple-element.99.dqkv_ref, bf16[8,2,64,4096]{3,2,1,0:T(8,128)(2,1)} %bitcast.79, bf16[256,4096]{1,0:T(8,128)(2,1)} %bitcast.77, f32[256,128]{1,0:T(8,128)} %get-tuple-element.87.ca_ref.c_ref, ...), custom_call_target="tpu_custom_call" | custom-call | tf_op jit(solution)/shard_map/lane_in_back/pallas_call | solution.py:908
  364.2 6.1 %reshape.389 = f32[2,128,4,1024]{3,2,1,0:T(4,128)} reshape(f32[256,4096]{1,0:T(8,128)} %get-tuple-element.103) | data formatting | bytes 8388608 | tf_op jit(solution)/shard_map/reshape | solution.py:1320
  370.4 2.0 select_bitcast_fusion.1
  374.1 2.0 collective-permute-start.5
  376.1 1.5 collective-permute-start.6
  377.6 2.7 collective-permute-done.6
  380.4 10.9 %collective-permute-done.4 = bf16[704,512]{1,0:T(8,128)(2,1)S(1)} collective-permute-done((bf16[704,512]{1,0:T(8,128)(2,1)}, bf16[704,512]{1,0:T(8,128)(2,1)S(1)}, u32[]{:S(2)}, u32[]{:S(2)}) %collective-permute-start.4) | collective-permute-done | bytes 720928 | tf_op jit(solution)/shard_map/ppermute | solution.py:1090
  391.2 1.7 collective-permute-done.5
  392.9 1.7 convert_add_fusion
  395.8 2.3 collective-permute-start.8
  399.7 7.6 %collective-permute-done.9 = f32[116,128]{1,0:T(8,128)S(1)} collective-permute-done((f32[116,128]{1,0:T(8,128)S(1)}, f32[116,128]{1,0:T(8,128)S(1)}, u32[]{:S(2)}, u32[]{:S(2)}) %collective-permute-start.9) | collective-permute-done | bytes 59424 | tf_op jit(solution)/shard_map/ppermute | solution.py:1073
  409.6 1.7 collective-permute-start.10
  411.4 2.3 collective-permute-start.12
  413.7 3.5 collective-permute-done.12
  417.9 2.3 collective-permute-start.14
  420.2 3.6 reduce-scatter.5.cloned.1.call-done
  423.8 1.3 select_bitcast_fusion.2
  425.2 1.7 collective-permute-start.16
  426.8 2.2 collective-permute-start.17
  431.2 7.9 %collective-permute-done.13 = bf16[176,512]{1,0:T(8,128)(2,1)S(1)} collective-permute-done((bf16[176,512]{1,0:T(8,128)(2,1)S(1)}, bf16[176,512]{1,0:T(8,128)(2,1)S(1)}, u32[]{:S(2)}, u32[]{:S(2)}) %collective-permute-start.13) | collective-permute-done | bytes 180256 | tf_op jit(solution)/shard_map/ppermute | solution.py:1117
  439.1 1.3 collective-permute-start.20
  440.4 1.6 collective-permute-start.19
  442.1 2.2 collective-permute-start.18
  445.1 2.0 collective-permute-start.22
  448.5 6.3 %collective-permute-done.21 = bf16[16,4096]{1,0:T(8,128)(2,1)S(1)} collective-permute-done((bf16[16,4096]{1,0:T(8,128)(2,1)S(1)}, bf16[16,4096]{1,0:T(8,128)(2,1)S(1)}, u32[]{:S(2)}, u32[]{:S(2)}) %collective-permute-start.21) | collective-permute-done | bytes 131104 | tf_op jit(solution)/shard_map/ppermute | solution.py:1078
  455.0 2.1 collective-permute-start.25
  457.3 1.8 collective-permute-start.27
  459.1 1.6 collective-permute-start.26
  460.7 3.9 collective-permute-done.26
  465.4 1.6 collective-permute-done.24
  467.4 2.5 collective-permute-start.30
  471.7 1.4 maximum_maximum_fusion.x_ref
  473.1 3.0 split_rows.1
  478.7 2.1 ungroup_columns.1
  (193 shorter events, 31.1 us)
Async XLA Ops:
  7.2 66.1 %all-gather.5.cloned.1.call-start = ((), (), s32[]{:S(2)}) async-start(), calls=%async_computation.8 | async-start | bytes 9437184 | tf_op jit(solution)/shard_map/all_gather | solution.py:1107
  9.1 12.2 %copy-start.3 = (bf16[64,4096]{1,0:T(8,128)(2,1)S(1)}, bf16[64,4096]{1,0:T(8,128)(2,1)}, u32[]{:S(2)}) copy-start(bf16[64,4096]{1,0:T(8,128)(2,1)} %group_columns.1) | copy-start | bytes 1572868
  10.3 8.4 %collective-permute-start = (bf16[64,2048]{1,0:T(8,128)(2,1)S(1)}, bf16[64,2048]{1,0:T(8,128)(2,1)S(1)}, u32[]{:S(2)}, u32[]{:S(2)}) collective-permute-start(bf16[64,2048]{1,0:T(8,128)(2,1)S(1)} %get-tuple-element.179), channel_id=1, source_target_pairs={{0,8},{1,9},{2,10},{3,11},{4,12},{5,13},{6,14},{7,15},{8,0},{9,1},... | collective-permute-start | bytes 786440 | tf_op jit(solution)/shard_map/ppermute | solution.py:1090
  12.3 9.0 %collective-permute-start.1 = (bf16[64,2048]{1,0:T(8,128)(2,1)S(1)}, bf16[64,2048]{1,0:T(8,128)(2,1)S(1)}, u32[]{:S(2)}, u32[]{:S(2)}) collective-permute-start(bf16[64,2048]{1,0:T(8,128)(2,1)S(1)} %get-tuple-element.178), channel_id=1, source_target_pairs={{0,72},{1,73},{2,74},{3,75},{4,76},{5,77},{6,78},{7,79},{8,64},{9,... | collective-permute-start | bytes 786440 | tf_op jit(solution)/shard_map/ppermute | solution.py:1090
  21.4 1.2 copy-start.13
  21.4 1.2 copy-start.9
  22.5 1.1 copy-start.11
  22.6 164.5 %all-gather.7.cloned.1.call-start = ((), (), s32[]{:S(2)}) async-start(), calls=%async_computation.9 | async-start | bytes 25952256 | tf_op jit(solution)/shard_map/all_gather | solution.py:1107
  23.8 16.8 %collective-permute-start.2 = (bf16[704,512]{1,0:T(8,128)(2,1)S(1)}, bf16[704,512]{1,0:T(8,128)(2,1)S(1)}, u32[]{:S(2)}, u32[]{:S(2)}) collective-permute-start(bf16[704,512]{1,0:T(8,128)(2,1)S(1)} %get-tuple-element.165), channel_id=1, source_target_pairs={{0,8},{1,9},{2,10},{3,11},{4,12},{5,13},{6,14},{7,15},{8,0},{9,1},... | collective-permute-start | bytes 2162696 | tf_op jit(solution)/shard_map/ppermute | solution.py:1090
  24.5 17.9 %collective-permute-start.3 = (bf16[704,512]{1,0:T(8,128)(2,1)S(1)}, bf16[704,512]{1,0:T(8,128)(2,1)S(1)}, u32[]{:S(2)}, u32[]{:S(2)}) collective-permute-start(bf16[704,512]{1,0:T(8,128)(2,1)S(1)} %get-tuple-element.166), channel_id=1, source_target_pairs={{0,72},{1,73},{2,74},{3,75},{4,76},{5,77},{6,78},{7,79},{8,64},{9,... | collective-permute-start | bytes 2162696 | tf_op jit(solution)/shard_map/ppermute | solution.py:1090
  48.7 3.9 copy-start.29
  48.7 4.6 copy-start.2
  136.8 4.4 copy-start.8
  136.8 21.0 %all-to-all-start.1 = ((bf16[8,256,256]{2,1,0:T(8,128)(2,1)}), bf16[8,256,256]{2,1,0:T(8,128)(2,1)S(1)}, u32[]{:S(2)}, u32[]{:S(2)}) async-start(bf16[8,256,256]{2,1,0:T(8,128)(2,1)} %bitcast.89), calls=%async_computation.1 | async-start | bytes 2097152 | tf_op jit(solution)/shard_map/all_to_all | solution.py:1282
  140.5 229.8 %reduce-scatter.3.cloned.1.call-start = ((), (), s32[]{:S(2)}) async-start(), calls=%async_computation.6 | async-start | bytes 25952256 | tf_op jit(solution)/shard_map/reduce_scatter | solution.py:1111
  141.2 2.2 copy-start.30
  157.8 29.3 %copy-start = (bf16[8,256,256]{2,1,0:T(8,128)(2,1)}, bf16[8,256,256]{2,1,0:T(8,128)(2,1)S(1)}, u32[]{:S(2)}) copy-start(bf16[8,256,256]{2,1,0:T(8,128)(2,1)S(1)} %all-to-all-done.1.o_ref) | copy-start | bytes 3145732
  246.9 1.2 copy-start.12
  299.2 3.8 copy-start.25
  299.2 3.9 copy-start.24
  299.2 3.9 copy-start.26
  299.2 32.3 %all-to-all-start.3 = ((bf16[8,256,512]{2,1,0:T(8,128)(2,1)}), bf16[8,256,512]{2,1,0:T(8,128)(2,1)S(1)}, u32[]{:S(2)}, u32[]{:S(2)}) async-start(bf16[8,256,512]{2,1,0:T(8,128)(2,1)} %bitcast.84), calls=%async_computation.3 | async-start | bytes 4194304 | tf_op jit(solution)/shard_map/all_to_all | solution.py:1302
  303.0 120.8 %reduce-scatter.5.cloned.1.call-start = ((), (), s32[]{:S(2)}) async-start(), calls=%async_computation.7 | async-start | bytes 9437184 | tf_op jit(solution)/shard_map/reduce_scatter | solution.py:1111
  331.5 1.4 copy-start.1
  345.2 17.4 %copy-start.28 = (f32[8,128]{1,0:T(8,128)S(1)}, f32[8,128]{1,0:T(8,128)}, u32[]{:S(2)}) copy-start(f32[8,128]{1,0:T(8,128)} %get-tuple-element.107) | copy-start | bytes 12292
  345.2 17.4 %copy-start.27 = (f32[8,128]{1,0:T(8,128)S(1)}, f32[8,128]{1,0:T(8,128)}, u32[]{:S(2)}) copy-start(f32[8,128]{1,0:T(8,128)} %get-tuple-element.108) | copy-start | bytes 12292
  373.3 17.9 %collective-permute-start.4 = (bf16[704,512]{1,0:T(8,128)(2,1)}, bf16[704,512]{1,0:T(8,128)(2,1)S(1)}, u32[]{:S(2)}, u32[]{:S(2)}) collective-permute-start(bf16[704,512]{1,0:T(8,128)(2,1)} %get-tuple-element.164), channel_id=1, source_target_pairs={{0,8},{1,9},{2,10},{3,11},{4,12},{5,13},{6,14},{7,15},{8,0},{9,1},... | collective-permute-start | bytes 2162696 | tf_op jit(solution)/shard_map/ppermute | solution.py:1090
  374.1 18.8 %collective-permute-start.5 = (bf16[704,512]{1,0:T(8,128)(2,1)S(1)}, bf16[704,512]{1,0:T(8,128)(2,1)}, u32[]{:S(2)}, u32[]{:S(2)}) collective-permute-start(bf16[704,512]{1,0:T(8,128)(2,1)S(1)} %get-tuple-element.163), channel_id=1, source_target_pairs={{0,72},{1,73},{2,74},{3,75},{4,76},{5,77},{6,78},{7,79},{8,64},{9,... | collective-permute-start | bytes 2162696 | tf_op jit(solution)/shard_map/ppermute | solution.py:1090
  376.1 4.2 collective-permute-start.6
  391.2 1.7 copy-start.14
  394.6 1.1 copy-start.4
  395.8 11.5 %collective-permute-start.8 = (bf16[352,512]{1,0:T(8,128)(2,1)S(1)}, bf16[352,512]{1,0:T(8,128)(2,1)S(1)}, u32[]{:S(2)}, u32[]{:S(2)}) collective-permute-start(bf16[352,512]{1,0:T(8,128)(2,1)S(1)} %dynamic-slice_convert_fusion), channel_id=1, source_target_pairs={{0,48},{16,32},{32,16},{48,0},{64,112},{80,96},{96,80},{112,64},{1... | collective-permute-start | bytes 1081352 | tf_op jit(solution)/shard_map/ppermute | solution.py:1073
  398.1 9.1 %collective-permute-start.7 = (bf16[352,512]{1,0:T(8,128)(2,1)S(1)}, bf16[352,512]{1,0:T(8,128)(2,1)S(1)}, u32[]{:S(2)}, u32[]{:S(2)}) collective-permute-start(bf16[352,512]{1,0:T(8,128)(2,1)S(1)} %dynamic-slice_convert_fusion.1), channel_id=1, source_target_pairs={{0,16},{16,0},{32,48},{48,32},{64,80},{80,64},{96,112},{112,96},{1... | collective-permute-start | bytes 1081352 | tf_op jit(solution)/shard_map/ppermute | solution.py:1073
  398.5 8.8 %collective-permute-start.9 = (f32[116,128]{1,0:T(8,128)S(1)}, f32[116,128]{1,0:T(8,128)S(1)}, u32[]{:S(2)}, u32[]{:S(2)}) collective-permute-start(f32[116,128]{1,0:T(8,128)S(1)} %add.167), channel_id=1, source_target_pairs={{0,48},{16,32},{32,16},{48,0},{64,112},{80,96},{96,80},{112,64},{1... | collective-permute-start | bytes 178184 | tf_op jit(solution)/shard_map/ppermute | solution.py:1073
  408.5 8.6 %collective-permute-start.11 = (bf16[176,512]{1,0:T(8,128)(2,1)S(1)}, bf16[176,512]{1,0:T(8,128)(2,1)S(1)}, u32[]{:S(2)}, u32[]{:S(2)}) collective-permute-start(bf16[176,512]{1,0:T(8,128)(2,1)S(1)} %dynamic-slice_convert_fusion.2), channel_id=1, source_target_pairs={{0,16},{16,0},{32,48},{48,32},{64,80},{80,64},{96,112},{112,96},{1... | collective-permute-start | bytes 540680 | tf_op jit(solution)/shard_map/ppermute | solution.py:1073
  409.6 7.5 %collective-permute-start.10 = (bf16[176,512]{1,0:T(8,128)(2,1)S(1)}, bf16[176,512]{1,0:T(8,128)(2,1)S(1)}, u32[]{:S(2)}, u32[]{:S(2)}) collective-permute-start(bf16[176,512]{1,0:T(8,128)(2,1)S(1)} %dynamic-slice_convert_fusion.3), channel_id=1, source_target_pairs={{0,48},{16,32},{32,16},{48,0},{64,112},{80,96},{96,80},{112,64},{1... | collective-permute-start | bytes 540680 | tf_op jit(solution)/shard_map/ppermute | solution.py:1073
  411.4 5.8 %collective-permute-start.12 = (f32[116,128]{1,0:T(8,128)S(1)}, f32[116,128]{1,0:T(8,128)S(1)}, u32[]{:S(2)}, u32[]{:S(2)}) collective-permute-start(f32[116,128]{1,0:T(8,128)S(1)} %add.174), channel_id=1, source_target_pairs={{0,64},{16,80},{32,96},{48,112},{64,0},{80,16},{96,32},{112,48},{1... | collective-permute-start | bytes 178184 | tf_op jit(solution)/shard_map/ppermute | solution.py:1117
  417.9 11.1 %copy-start.7 = (f32[352,512]{1,0:T(8,128)S(1)}, f32[352,512]{1,0:T(8,128)}, u32[]{:S(2)}) copy-start(f32[352,512]{1,0:T(8,128)} %copy-done.6) | copy-start | bytes 2162692
  417.9 13.3 %collective-permute-start.14 = (bf16[176,512]{1,0:T(8,128)(2,1)S(1)}, bf16[176,512]{1,0:T(8,128)(2,1)S(1)}, u32[]{:S(2)}, u32[]{:S(2)}) collective-permute-start(bf16[176,512]{1,0:T(8,128)(2,1)S(1)} %add_convert_fusion.2), channel_id=1, source_target_pairs={{0,64},{16,80},{32,96},{48,112},{64,0},{80,16},{96,32},{112,48},{1... | collective-permute-start | bytes 540680 | tf_op jit(solution)/shard_map/ppermute | solution.py:1117
  423.8 5.2 %copy-start.17 = (bf16[176,512]{1,0:T(8,128)(2,1)S(1)}, bf16[176,512]{1,0:T(8,128)(2,1)}, u32[]{:S(2)}) copy-start(bf16[176,512]{1,0:T(8,128)(2,1)} %copy-done.16) | copy-start | bytes 540676
  425.1 19.1 %copy-start.5 = (bf16[1,2,64,4096]{3,2,1,0:T(8,128)(2,1)S(1)}, bf16[1,2,64,4096]{3,2,1,0:T(8,128)(2,1)}, u32[]{:S(2)}) copy-start(bf16[1,2,64,4096]{3,2,1,0:T(8,128)(2,1)} %reduce-scatter.5.cloned.1.call-done) | copy-start | bytes 3145732
  425.2 13.9 %collective-permute-start.16 = (bf16[64,2048]{1,0:T(8,128)(2,1)S(1)}, bf16[64,2048]{1,0:T(8,128)(2,1)S(1)}, u32[]{:S(2)}, u32[]{:S(2)}) collective-permute-start(bf16[64,2048]{1,0:T(8,128)(2,1)S(1)} %get-tuple-element.177), channel_id=1, source_target_pairs={{0,8},{1,9},{2,10},{3,11},{4,12},{5,13},{6,14},{7,15},{8,0},{9,1},... | collective-permute-start | bytes 786440 | tf_op jit(solution)/shard_map/ppermute | solution.py:1090
  426.8 12.3 %collective-permute-start.17 = (bf16[64,2048]{1,0:T(8,128)(2,1)S(1)}, bf16[64,2048]{1,0:T(8,128)(2,1)S(1)}, u32[]{:S(2)}, u32[]{:S(2)}) collective-permute-start(bf16[64,2048]{1,0:T(8,128)(2,1)S(1)} %get-tuple-element.176), channel_id=1, source_target_pairs={{0,72},{1,73},{2,74},{3,75},{4,76},{5,77},{6,78},{7,79},{8,64},{9,... | collective-permute-start | bytes 786440 | tf_op jit(solution)/shard_map/ppermute | solution.py:1090
  429.0 10.1 %collective-permute-start.13 = (bf16[176,512]{1,0:T(8,128)(2,1)S(1)}, bf16[176,512]{1,0:T(8,128)(2,1)S(1)}, u32[]{:S(2)}, u32[]{:S(2)}) collective-permute-start(bf16[176,512]{1,0:T(8,128)(2,1)S(1)} %add_convert_fusion.3), channel_id=1, source_target_pairs={{0,64},{16,80},{32,96},{48,112},{64,0},{80,16},{96,32},{112,48},{1... | collective-permute-start | bytes 540680 | tf_op jit(solution)/shard_map/ppermute | solution.py:1117
  429.8 1.3 collective-permute-start.15
  439.1 8.0 %collective-permute-start.20 = (f32[116,128]{1,0:T(8,128)S(1)}, f32[116,128]{1,0:T(8,128)S(1)}, u32[]{:S(2)}, u32[]{:S(2)}) collective-permute-start(f32[116,128]{1,0:T(8,128)S(1)} %add.184), channel_id=1, source_target_pairs={{0,2},{1,3},{2,0},{3,1},{4,6},{5,7},{6,4},{7,5},{8,10},{9,11},{10,... | collective-permute-start | bytes 178184 | tf_op jit(solution)/shard_map/ppermute | solution.py:1186
  440.4 14.4 %collective-permute-start.19 = (bf16[176,512]{1,0:T(8,128)(2,1)S(1)}, bf16[176,512]{1,0:T(8,128)(2,1)S(1)}, u32[]{:S(2)}, u32[]{:S(2)}) collective-permute-start(bf16[176,512]{1,0:T(8,128)(2,1)S(1)} %add_convert_fusion), channel_id=1, source_target_pairs={{0,16},{16,0},{32,48},{48,32},{64,80},{80,64},{96,112},{112,96},{1... | collective-permute-start | bytes 540680 | tf_op jit(solution)/shard_map/ppermute | solution.py:1073
  442.1 12.8 %collective-permute-start.18 = (bf16[176,512]{1,0:T(8,128)(2,1)S(1)}, bf16[176,512]{1,0:T(8,128)(2,1)S(1)}, u32[]{:S(2)}, u32[]{:S(2)}) collective-permute-start(bf16[176,512]{1,0:T(8,128)(2,1)S(1)} %add_convert_fusion.1), channel_id=1, source_target_pairs={{0,48},{16,32},{32,16},{48,0},{64,112},{80,96},{96,80},{112,64},{1... | collective-permute-start | bytes 540680 | tf_op jit(solution)/shard_map/ppermute | solution.py:1073
  444.5 10.4 %collective-permute-start.21 = (bf16[16,4096]{1,0:T(8,128)(2,1)S(1)}, bf16[16,4096]{1,0:T(8,128)(2,1)S(1)}, u32[]{:S(2)}, u32[]{:S(2)}) collective-permute-start(bf16[16,4096]{1,0:T(8,128)(2,1)S(1)} %get-tuple-element.169), channel_id=1, source_target_pairs={{0,16},{16,32},{32,48},{48,0},{64,80},{80,96},{96,112},{112,64},{1... | collective-permute-start | bytes 393224 | tf_op jit(solution)/shard_map/ppermute | solution.py:1078
  445.1 9.7 %collective-permute-start.22 = (bf16[16,4096]{1,0:T(8,128)(2,1)S(1)}, bf16[16,4096]{1,0:T(8,128)(2,1)S(1)}, u32[]{:S(2)}, u32[]{:S(2)}) collective-permute-start(bf16[16,4096]{1,0:T(8,128)(2,1)S(1)} %get-tuple-element.168), channel_id=1, source_target_pairs={{0,32},{16,48},{32,0},{48,16},{64,96},{80,112},{96,64},{112,80},{1... | collective-permute-start | bytes 393224 | tf_op jit(solution)/shard_map/ppermute | solution.py:1078
  447.8 7.1 %collective-permute-start.23 = (bf16[16,4096]{1,0:T(8,128)(2,1)S(1)}, bf16[16,4096]{1,0:T(8,128)(2,1)S(1)}, u32[]{:S(2)}, u32[]{:S(2)}) collective-permute-start(bf16[16,4096]{1,0:T(8,128)(2,1)S(1)} %get-tuple-element.167), channel_id=1, source_target_pairs={{0,48},{16,0},{32,16},{48,32},{64,112},{80,64},{96,80},{112,96},{1... | collective-permute-start | bytes 393224 | tf_op jit(solution)/shard_map/ppermute | solution.py:1078
  454.9 4.2 copy-start.22
  455.0 10.4 %collective-permute-start.25 = (bf16[352,512]{1,0:T(8,128)(2,1)S(1)}, bf16[352,512]{1,0:T(8,128)(2,1)S(1)}, u32[]{:S(2)}, u32[]{:S(2)}) collective-permute-start(bf16[352,512]{1,0:T(8,128)(2,1)S(1)} %pad_maximum_fusion.4), channel_id=1, source_target_pairs={{0,48},{16,32},{32,16},{48,0},{64,112},{80,96},{96,80},{112,64},{1... | collective-permute-start | bytes 1081352 | tf_op jit(solution)/shard_map/ppermute | solution.py:1073
  457.1 9.8 %collective-permute-start.24 = (bf16[352,512]{1,0:T(8,128)(2,1)S(1)}, bf16[352,512]{1,0:T(8,128)(2,1)S(1)}, u32[]{:S(2)}, u32[]{:S(2)}) collective-permute-start(bf16[352,512]{1,0:T(8,128)(2,1)S(1)} %pad_maximum_fusion.3), channel_id=1, source_target_pairs={{0,16},{16,0},{32,48},{48,32},{64,80},{80,64},{96,112},{112,96},{1... | collective-permute-start | bytes 1081352 | tf_op jit(solution)/shard_map/ppermute | solution.py:1073
  457.3 7.3 %collective-permute-start.27 = (bf16[16,4096]{1,0:T(8,128)(2,1)S(1)}, bf16[16,4096]{1,0:T(8,128)(2,1)S(1)}, u32[]{:S(2)}, u32[]{:S(2)}) collective-permute-start(bf16[16,4096]{1,0:T(8,128)(2,1)S(1)} %add_convert_fusion.5), channel_id=1, source_target_pairs={{0,64},{16,80},{32,96},{48,112},{64,0},{80,16},{96,32},{112,48},{1... | collective-permute-start | bytes 393224 | tf_op jit(solution)/shard_map/ppermute | solution.py:1117
  459.1 5.5 %collective-permute-start.26 = (f32[116,128]{1,0:T(8,128)S(1)}, f32[116,128]{1,0:T(8,128)S(1)}, u32[]{:S(2)}, u32[]{:S(2)}) collective-permute-start(f32[116,128]{1,0:T(8,128)S(1)} %add.197), channel_id=1, source_target_pairs={{0,6},{1,7},{2,4},{3,5},{4,2},{5,3},{6,0},{7,1},{8,14},{9,15},{10,... | collective-permute-start | bytes 178184 | tf_op jit(solution)/shard_map/ppermute | solution.py:1186
  467.0 4.7 copy-start.15
  467.0 9.0 %collective-permute-start.29 = (bf16[16,4096]{1,0:T(8,128)(2,1)S(1)}, bf16[16,4096]{1,0:T(8,128)(2,1)S(1)}, u32[]{:S(2)}, u32[]{:S(2)}) collective-permute-start(bf16[16,4096]{1,0:T(8,128)(2,1)S(1)} %add_convert_fusion.4.refs_0_), channel_id=1, source_target_pairs={{0,16},{16,32},{32,48},{48,0},{64,80},{80,96},{96,112},{112,64},{1... | collective-permute-start | bytes 393224 | tf_op jit(solution)/shard_map/ppermute | solution.py:1078
  467.4 8.7 %collective-permute-start.30 = (bf16[16,4096]{1,0:T(8,128)(2,1)S(1)}, bf16[16,4096]{1,0:T(8,128)(2,1)S(1)}, u32[]{:S(2)}, u32[]{:S(2)}) collective-permute-start(bf16[16,4096]{1,0:T(8,128)(2,1)S(1)} %add_convert_fusion.4.refs_0_), channel_id=1, source_target_pairs={{0,32},{16,48},{32,0},{48,16},{64,96},{80,112},{96,64},{112,80},{1... | collective-permute-start | bytes 393224 | tf_op jit(solution)/shard_map/ppermute | solution.py:1078
  469.9 6.2 %collective-permute-start.31 = (bf16[16,4096]{1,0:T(8,128)(2,1)S(1)}, bf16[16,4096]{1,0:T(8,128)(2,1)S(1)}, u32[]{:S(2)}, u32[]{:S(2)}) collective-permute-start(bf16[16,4096]{1,0:T(8,128)(2,1)S(1)} %add_convert_fusion.4.refs_0_), channel_id=1, source_target_pairs={{0,48},{16,0},{32,16},{48,32},{64,112},{80,64},{96,80},{112,96},{1... | collective-permute-start | bytes 393224 | tf_op jit(solution)/shard_map/ppermute | solution.py:1078
  470.3 5.7 %collective-permute-start.28 = (f32[116,128]{1,0:T(8,128)S(1)}, f32[116,128]{1,0:T(8,128)S(1)}, u32[]{:S(2)}, u32[]{:S(2)}) collective-permute-start(f32[116,128]{1,0:T(8,128)S(1)} %add.199), channel_id=1, source_target_pairs={{0,8},{1,9},{2,10},{3,11},{4,12},{5,13},{6,14},{7,15},{8,0},{9,1},... | collective-permute-start | bytes 178184 | tf_op jit(solution)/shard_map/ppermute | solution.py:1117
  476.0 2.7 copy-start.18
  476.1 2.7 copy-start.19
  476.1 2.7 copy-start.20
  (5 other events, 4.0 us)
Sparse Core Ops, SparseCore 0:
  22.7 50.5 all-gather.4
  75.5 111.5 all-gather.6
  247.1 122.3 reduce-scatter.2
  371.7 52.0 reduce-scatter.4
